TPU v7x, 32 devices: a whole 2x2x4 slice. The times are simulated.
32 devices in a mesh: seq: 16 (over z, y, x), head: 2 (over core).
Axes of the slice: x: 2, y: 2, z: 4, core: 2. Of those that a mesh axis runs over, the one named last changes fastest.
Arguments:
- hidden: bfloat16 [2048, 2048], P('seq'), may hold values from -6 to 6
- queries: bfloat16 [2048, 3072], P('seq', 'head'), may hold values from -90 to 90
- req_len: int32 [2], replicated, may hold values from 1 to 1920, 2048 in all
- req_offset: int32 [2], replicated, may hold values from 0 to 4095
- expert_ids: int32 [2048, 6], P('seq'), may hold values from 0 to 15, all different within a row; in each aligned block of 128 rows (0 to 127, 128 to 255, ...) at most 64 rows name the same one
- decode_slot: int32 [128], replicated, may hold values from 0 to 127, as said below
- attn_gain: float32 [2048], replicated, may hold values from 0.25 to 1.75
- kv_down: bfloat16 [2048, 576], replicated, may hold values from -0.125 to 0.125
- kv_gain: float32 [512], replicated, may hold values from 0.25 to 1.75
- key_up: bfloat16 [16, 128, 512], P('head'), may hold values from -0.5 to 0.5
- value_up: bfloat16 [16, 512, 128], P('head'), may hold values from -0.25 to 0.25
- out_proj: bfloat16 [2048, 2048], P('head'), may hold values from -0.5 to 0.5
- ffn_gain: float32 [2048], replicated, may hold values from 0.25 to 1.75
- router: float32 [2048, 16], replicated, may hold values from -0.125 to 0.125
- expert_gate_up: bfloat16 [16, 2, 2048, 1408], P('seq', None, None, 'head'), may hold values from -0.125 to 0.125
- expert_down: bfloat16 [16, 1408, 2048], P('seq', 'head'), may hold values from -0.15625 to 0.15625
Outputs:
- output: bfloat16 [2048, 2048], P('seq', 'head')
- decode_latent: bfloat16 [128, 16, 512], P(('seq', 'head'))
- decode_rope: bfloat16 [128, 1024], P(('seq', 'head'))
Inputs may be any that keep to these rules, and one draw needn't show every extreme that they name: `req_len`: the lengths sum to 2048. `expert_ids`: the 128 rows of one index of seq name one expert at most 64 times in all. `decode_slot`: all entries differ; slot g belongs to device g // 4 in the order seq then head, and all 4 slots of some device are named.
All inputs are finite; a program needn't handle non-finite values.
Results may differ from a plain program's by a relative error of at most 0.02.
Values may be sent and summed in bfloat16 or wider, within the bound.
A program may use at most 128 MiB of HBM per device.

v0:
```python
import functools
import math

import jax
import jax.numpy as jnp
from jax import lax
from jax.experimental import pallas as pl
from jax.experimental.pallas import tpu as pltpu
from jax.sharding import PartitionSpec as P

D = 2048
NOPE = 128
ROPE = 64
V_HEAD = 128
KV_RANK = 512
TOP = 6
BLOCK = 16
DEC_SLOTS = 4


ROPE_BASE = 50000.0
ROUTE_SCALE = 2.446
EPSILON = 1e-06
MASKED = -1e30


def rms_rows(values, scale_gain):
    values = values.astype(jnp.float32)
    inverse = lax.rsqrt(jnp.mean(values * values, axis=-1, keepdims=True) + EPSILON)
    return values * inverse * scale_gain


def angles(position, rope_width):
    half_width = rope_width // 2
    freq_steps = jnp.arange(half_width).astype(jnp.float32) * (2.0 / rope_width)
    frequency = jnp.exp(-math.log(ROPE_BASE) * freq_steps)
    return position.astype(jnp.float32)[:, None] * frequency[None, :]


def rotate(values, rot_angle):
    half_width = values.shape[-1] // 2
    first_half = values[..., :half_width].astype(jnp.float32)
    second_half = values[..., half_width:].astype(jnp.float32)
    cosine = jnp.cos(rot_angle)
    sine_part = jnp.sin(rot_angle)
    return jnp.concatenate(
        [
            first_half * cosine - second_half * sine_part,
            first_half * sine_part + second_half * cosine,
        ],
        axis=-1,
    )


def running(lengths):
    index = jnp.arange(lengths.shape[0])
    return jnp.sum(jnp.where(index[None, :] <= index[:, None], lengths[None, :], 0), axis=1)


def ranks(member):
    count = member.shape[-1]
    index = jnp.arange(count)
    before = (index[:, None] < index[None, :]).astype(jnp.bfloat16)
    return jnp.dot(member, before, preferred_element_type=jnp.float32).astype(jnp.int32)


def request_of(req_len, token_index):
    req_ends = running(req_len)
    return jnp.sum((token_index[:, None] >= req_ends[None, :]).astype(jnp.int32), axis=1)


def position_of(req_len, req_offset, token_index):
    request = request_of(req_len, token_index)
    req_ends = running(req_len)
    starts = req_ends - req_len
    member = request[:, None] == jnp.arange(req_len.shape[0])[None, :]
    start_at = jnp.sum(jnp.where(member, starts[None, :], 0), axis=1)
    offset = jnp.sum(jnp.where(member, req_offset[None, :], 0), axis=1)
    return offset + token_index - start_at


def key_width(piece_rows):
    for option_width in (1024, 512, 256, 128):
        return option_width
    return piece_rows


MESH = pl.DeviceIdType.MESH


def flip(place, step):
    return place + step * (1 - 2 * lax.rem(lax.div(place, step), 2))


def place_of(s, h, nz, back, turn):
    line = lax.rem(lax.div(s, 4) - back + nz, nz)
    block = line * 4 + lax.rem(s, 4)
    if turn & 1:
        block = flip(block, 2 - h)
    if turn & 2:
        block = flip(block, 1 + h)
    return block


def meet(s, h, nz):
    barrier = pltpu.get_barrier_semaphore()
    peers = [(place_of(s, h, nz, back, 0), h) for back in range(1, nz)]
    peers += [(flip(s, 2 - h), h), (flip(s, 1 + h), h), (s, 1 - h)]
    for peer in peers:
        pl.semaphore_signal(barrier, inc=1, device_id=peer, device_id_type=MESH)
    pl.semaphore_wait(barrier, len(peers))


class Spread:
    def __init__(self, buf, s, h, nz, sems, blocks_first=False):
        self.blocks_first = blocks_first
        self.buf, self.s, self.h, self.nz = buf, s, h, nz
        self.sems = sems

    def move(self, block, kind, index, device):
        view = self.buf.at[block, self.h] if self.blocks_first else self.buf.at[self.h, block]
        return pltpu.make_async_remote_copy(
            src_ref=view,
            dst_ref=view,
            send_sem=self.sems[2 * kind].at[index],
            recv_sem=self.sems[2 * kind + 1].at[index],
            device_id=device,
            device_id_type=MESH,
        )

    def block(self, back, turn):
        return place_of(self.s, self.h, self.nz, back, turn)

    def line(self, ahead):
        device = (place_of(self.s, self.h, self.nz, self.nz - ahead, 0), self.h)
        return self.move(self.block(0, 0), 0, ahead, device)

    def line_in(self, back):
        return self.move(self.block(back, 0), 0, back, (self.s, 1 - self.h))

    def second(self, back, turn=0):
        return self.move(self.block(back, turn), 1, back, (flip(self.s, 2 - self.h), self.h))

    def third(self, back, side, turn=0):
        device = (flip(self.s, 1 + self.h), self.h)
        return self.move(self.block(back, turn + side), 2, 2 * back + side, device)

    def sibling(self, back, mine):
        half = self.h if mine else 1 - self.h
        line = lax.rem(lax.div(self.s, 4) - back + self.nz, self.nz)
        four = pl.ds(line * 4, 4)
        view = self.buf.at[four, half] if self.blocks_first else self.buf.at[half, four]
        return pltpu.make_async_remote_copy(
            src_ref=view,
            dst_ref=view,
            send_sem=self.sems[6].at[back],
            recv_sem=self.sems[7].at[back],
            device_id=(self.s, 1 - self.h),
            device_id_type=MESH,
        )

    def send_all(self):
        for ahead in range(1, self.nz):
            self.line(ahead).start()
        for back in range(self.nz):
            if back:
                self.line_in(back).wait_recv()
            self.third(back, 0).start()
            self.second(back).start()
            self.second(back, 1).wait_recv()
            self.third(back, 1).start()

    def pass_on(self, back):
        for side in range(2):
            self.third(back, side, 2).wait_recv()
        self.sibling(back, True).start()

    def drain(self):
        for ahead in range(1, self.nz):
            self.line(ahead).wait_send()
        for back in range(self.nz):
            self.second(back).wait_send()
            self.third(back, 0).wait_send()
            self.third(back, 1).wait_send()
            self.sibling(back, True).wait_send()


def spread_sems(nz):
    dma = pltpu.SemaphoreType.DMA
    return [dma((nz,)), dma((nz,)), dma((nz,)), dma((nz,)), dma((2 * nz,)), dma((2 * nz,)), dma((nz,)), dma((nz,))]


def gather_kernel(nz, rows_ref, out_ref, *sems):
    s, h = lax.axis_index("seq"), lax.axis_index("head")
    out_ref[s, h] = rows_ref[h]
    meet(s, h, nz)
    spread = Spread(out_ref, s, h, nz, sems, True)
    spread.send_all()
    for back in range(nz):
        spread.pass_on(back)
    for back in range(nz):
        spread.sibling(back, False).wait_recv()
    spread.drain()


def gather_rows(rows, seq_count):
    tok_rows, width = rows.shape
    nz = seq_count // 4
    out = pl.pallas_call(
        functools.partial(gather_kernel, nz),
        out_shape=jax.ShapeDtypeStruct((seq_count, 2, tok_rows // 2, width), rows.dtype),
        in_specs=[pl.BlockSpec(memory_space=pltpu.VMEM)],
        out_specs=pl.BlockSpec(memory_space=pltpu.VMEM),
        scratch_shapes=spread_sems(nz),
        compiler_params=pltpu.CompilerParams(
            collective_id=0, has_side_effects=True, vmem_limit_bytes=16 * 1024 * 1024
        ),
    )(rows.reshape(2, tok_rows // 2, width))
    return out.reshape(seq_count * tok_rows, width)


def expert_kernel(
    nz,
    hidden_ref,
    attn_ref,
    gain_ref,
    pick_ref,
    place_ref,
    chosen_ref,
    router_ref,
    gate_up_hbm,
    down_hbm,
    out_ref,
    attn_in,
    mixed,
    x_buf,
    part,
    sib_buf,
    t3_buf,
    t2_buf,
    t1_buf,
    gate_up,
    down,
    rows_buf,
    act_buf,
    res_buf,
    load_sem,
    attn_sem,
    e0_send,
    e0_recv,
    e3_send,
    e3_recv,
    e2_send,
    e2_recv,
    e1_send,
    e1_recv,
    *sems,
):
    s, h = lax.axis_index("seq"), lax.axis_index("head")
    cols = hidden_ref.shape[1]
    half = cols // 2
    slots = pick_ref.shape[1]
    loads = [
        pltpu.make_async_copy(gate_up_hbm, gate_up, load_sem.at[0]),
        pltpu.make_async_copy(down_hbm, down, load_sem.at[1]),
    ]
    for load in loads:
        load.start()
    meet(s, h, nz)
    swap = pltpu.make_async_remote_copy(
        src_ref=attn_ref,
        dst_ref=attn_in,
        send_sem=attn_sem.at[0],
        recv_sem=attn_sem.at[1],
        device_id=(s, 1 - h),
        device_id_type=MESH,
    )
    swap.start()
    swap.wait_recv()
    total = hidden_ref[...].astype(jnp.float32) + (
        attn_ref[...].astype(jnp.float32) + attn_in[...].astype(jnp.float32)
    )
    mixed[0] = total[:, :half]
    mixed[1] = total[:, half:]
    inverse = lax.rsqrt(jnp.mean(total * total, axis=1, keepdims=True) + EPSILON)
    x_buf[h, s] = (mixed[h] * inverse * gain_ref[h][None, :]).astype(jnp.bfloat16)
    spread = Spread(x_buf, s, h, nz, sems)
    spread.send_all()
    spread.pass_on(0)
    for load in loads:
        load.wait()

    def remote(src, dst, send, recv, index, device):
        return pltpu.make_async_remote_copy(
            src_ref=src,
            dst_ref=dst,
            send_sem=send.at[index],
            recv_sem=recv.at[index],
            device_id=device,
            device_id_type=MESH,
        )

    sibling = (s, 1 - h)
    partner2 = (flip(s, 2 - h), h)
    partner3 = (flip(s, 1 + h), h)

    def line_of(back):
        return lax.rem(lax.div(s, 4) - back + nz, nz)

    def give0(back):
        base = pl.ds(line_of(back) * 4, 4)
        return remote(part.at[1 - h, base], sib_buf.at[base], e0_send, e0_recv, back, sibling)

    def give3(back, side):
        block = place_of(s, h, nz, back, 2 + side)
        index = 2 * back + side
        return remote(part.at[h, block], t3_buf.at[index], e3_send, e3_recv, index, partner3)

    def give2(back):
        block = place_of(s, h, nz, back, 1)
        return remote(part.at[h, block], t2_buf.at[back], e2_send, e2_recv, back, partner2)

    def give1(back):
        block = place_of(s, h, nz, back, 0)
        return remote(part.at[h, block], t1_buf.at[back], e1_send, e1_recv, back, (block, h))

    def add(block, other):
        part[h, block] = (
            part[h, block].astype(jnp.float32) + other.astype(jnp.float32)
        ).astype(jnp.bfloat16)

    def feed(back):
        spread.sibling(back, False).wait_recv()
        base = line_of(back) * 4
        for c in range(4):
            pick = pick_ref[base + c]
            for side in range(2):
                rows_buf[c * slots : (c + 1) * slots, side * half : (side + 1) * half] = jnp.dot(
                    pick, x_buf[side, base + c], preferred_element_type=jnp.float32
                ).astype(jnp.bfloat16)
        rows = rows_buf[...]
        logit = jnp.dot(rows, router_ref[...], preferred_element_type=jnp.float32)
        width = logit.shape[1] // 3
        logit = logit[:, :width] + (logit[:, width : 2 * width] + logit[:, 2 * width :])
        score = 1.0 / (1.0 + jnp.exp(-logit))
        chosen = score * chosen_ref[pl.ds(base, 4)].reshape(4 * slots, width)
        own = jnp.where(lax.broadcasted_iota(jnp.int32, chosen.shape, 1) == s, chosen, 0.0)
        own = jnp.sum(own, axis=1, keepdims=True)
        every = jnp.sum(chosen, axis=1, keepdims=True)
        weight = ROUTE_SCALE * own / jnp.where(every > 0.0, every, 1.0)
        across = (((1,), (1,)), ((), ()))
        gate = lax.dot_general(rows, gate_up[0], across, preferred_element_type=jnp.float32)
        up = lax.dot_general(rows, gate_up[1], across, preferred_element_type=jnp.float32)
        act_buf[...] = (gate / (1.0 + jnp.exp(-gate)) * up * weight).astype(jnp.bfloat16)
        res_buf[...] = jnp.dot(
            act_buf[...], down[...], preferred_element_type=jnp.float32
        ).astype(jnp.bfloat16)
        for c in range(4):
            for side in range(2):
                part[side, base + c] = jnp.dot(
                    place_ref[base + c],
                    res_buf[c * slots : (c + 1) * slots, side * half : (side + 1) * half],
                    preferred_element_type=jnp.float32,
                ).astype(jnp.bfloat16)
        give0(back).start()

    def fold0(back):
        give0(back).wait_recv()
        for turn in (2, 3, 1, 0):
            block = place_of(s, h, nz, back, turn)
            add(block, sib_buf[block])
            if turn >= 2:
                give3(back, turn - 2).start()

    def fold3(back):
        for side in (1, 0):
            give3(back, side).wait_recv()
            add(place_of(s, h, nz, back, side), t3_buf[2 * back + side])
            if side:
                give2(back).start()

    def fold2(back):
        give2(back).wait_recv()
        add(place_of(s, h, nz, back, 0), t2_buf[back])

        @pl.when(back > 0)
        def _():
            give1(back).start()

    @pl.loop(0, nz + 3)
    def _(step):
        @pl.when(step < nz)
        def _():
            feed(step)

        @pl.when(step < nz - 1)
        def _():
            spread.pass_on(step + 1)

        @pl.when((step >= 3))
        def _():
            fold2(step - 3)

        @pl.when((step >= 2) & (step < nz + 2))
        def _():
            fold3(step - 2)

        @pl.when((step >= 1) & (step < nz + 1))
        def _():
            fold0(step - 1)

    result = mixed[h] + part[h, s].astype(jnp.float32)
    for back in range(1, nz):
        give1(back).wait_recv()
        result = result + t1_buf[back].astype(jnp.float32)
    out_ref[...] = result.astype(out_ref.dtype)
    swap.wait_send()
    spread.drain()
    for back in range(nz):
        give0(back).wait_send()
        give3(back, 0).wait_send()
        give3(back, 1).wait_send()
        give2(back).wait_send()
        if back:
            give1(back).wait_send()


def expert_layer(hidden, attn_part, masks, ffn_gain, router, gate_up, down, seq_place, seq_count):
    tok_rows, cols = hidden.shape
    half = cols // 2
    nz = seq_count // 4
    expert_count = router.shape[1]
    hidden_units = down.shape[0]
    capacity = max(2, tok_rows * TOP * 4 // (3 * expert_count))
    mine = lax.dynamic_index_in_dim(masks, seq_place, 2, keepdims=False)
    rank = ranks(mine)
    slot = jnp.arange(capacity, dtype=jnp.int32)
    pick = (rank[:, None, :] == slot[None, :, None]) & (mine[:, None, :] > 0)
    pick = pick.astype(jnp.bfloat16)
    place = (rank[:, :, None] == slot[None, None, :]) & (mine[:, :, None] > 0)
    place = place.astype(jnp.bfloat16)
    wide_masks = jnp.pad(masks, ((0, 0), (0, 0), (0, 128 - expert_count)))
    chosen = jnp.einsum("brt,bte->bre", pick, wide_masks, preferred_element_type=jnp.float32)
    router = jnp.pad(router, ((0, 0), (0, 128 - expert_count)))
    high = lax.reduce_precision(router, 8, 7)
    middle = lax.reduce_precision(router - high, 8, 7)
    low = router - high - middle
    router3 = jnp.concatenate([high, middle, low], axis=1).astype(jnp.bfloat16)
    vmem = pl.BlockSpec(memory_space=pltpu.VMEM)
    hbm = pl.BlockSpec(memory_space=pl.ANY)
    dma = pltpu.SemaphoreType.DMA
    bf16 = jnp.bfloat16
    return pl.pallas_call(
        functools.partial(expert_kernel, nz),
        out_shape=jax.ShapeDtypeStruct((tok_rows, half), bf16),
        in_specs=[vmem] * 7 + [hbm] * 2,
        out_specs=vmem,
        scratch_shapes=[
            pltpu.VMEM((tok_rows, cols), bf16),
            pltpu.VMEM((2, tok_rows, half), jnp.float32),
            pltpu.VMEM((2, seq_count, tok_rows, half), bf16),
            pltpu.VMEM((2, seq_count, tok_rows, half), bf16),
            pltpu.VMEM((seq_count, tok_rows, half), bf16),
            pltpu.VMEM((2 * nz, tok_rows, half), bf16),
            pltpu.VMEM((nz, tok_rows, half), bf16),
            pltpu.VMEM((nz, tok_rows, half), bf16),
            pltpu.VMEM(gate_up.shape, bf16),
            pltpu.VMEM(down.shape, bf16),
            pltpu.VMEM((4 * capacity, cols), bf16),
            pltpu.VMEM((4 * capacity, hidden_units), bf16),
            pltpu.VMEM((4 * capacity, cols), bf16),
            dma((2,)),
            dma((2,)),
            dma((nz,)),
            dma((nz,)),
            dma((2 * nz,)),
            dma((2 * nz,)),
            dma((nz,)),
            dma((nz,)),
            dma((nz,)),
            dma((nz,)),
        ]
        + spread_sems(nz),
        compiler_params=pltpu.CompilerParams(
            collective_id=1, has_side_effects=True, vmem_limit_bytes=56 * 1024 * 1024
        ),
    )(hidden, attn_part, ffn_gain.reshape(2, half), pick, place, chosen, router3, gate_up, down)


def attend_kernel(
    key_tile,
    span_ref,
    first_ref,
    nope_ref,
    rope_ref,
    keys_ref,
    key_up_ref,
    value_up_ref,
    out_proj_ref,
    out_ref,
    query,
    acc,
    peak,
    total,
    heads_buf,
):
    heads, tok_rows = nope_ref.shape[0], nope_ref.shape[1]
    group = 4
    group_rows = group * tok_rows
    score_scale = 1.0 / math.sqrt(NOPE + ROPE)
    contract = (((1,), (1,)), ((), ()))
    for head in range(heads):
        here = slice(head * tok_rows, (head + 1) * tok_rows)
        query[here, :KV_RANK] = jnp.dot(
            nope_ref[head], key_up_ref[head], preferred_element_type=jnp.float32
        ).astype(jnp.bfloat16)
        query[here, KV_RANK:] = rope_ref[head]
    first = jnp.concatenate([first_ref[...]] * group, axis=0)
    own = span_ref[2] + lax.broadcasted_iota(jnp.int32, (tok_rows, 1), 0)
    own = jnp.concatenate([own] * group, axis=0)

    @pl.loop(0, heads // group)
    def _(part_no):
        base = pl.multiple_of(part_no * group_rows, group_rows)
        here = pl.ds(base, group_rows)
        peak[...] = jnp.full_like(peak, MASKED)
        total[...] = jnp.zeros_like(total)
        acc[...] = jnp.zeros_like(acc)

        @pl.loop(span_ref[0], span_ref[1])
        def _(tile):
            start = pl.multiple_of(tile * key_tile, key_tile)
            keys = keys_ref[pl.ds(start, key_tile), :]
            scores = score_scale * lax.dot_general(
                query[here, :], keys, contract, preferred_element_type=jnp.float32
            )
            index = start + lax.broadcasted_iota(jnp.int32, scores.shape, 1)
            allowed = (index <= own) & (index >= first)
            scores = jnp.where(allowed, scores, MASKED)
            old = peak[:, :1]
            new = jnp.maximum(old, jnp.max(scores, axis=1, keepdims=True))
            terms = jnp.where(allowed, jnp.exp(scores - new), 0.0)
            fade = jnp.exp(old - new)
            total[:, :1] = total[:, :1] * fade + jnp.sum(terms, axis=1, keepdims=True)
            peak[:, :1] = new
            acc[...] = acc[...] * fade + jnp.dot(
                terms.astype(jnp.bfloat16), keys[:, :KV_RANK], preferred_element_type=jnp.float32
            )

        attended = (acc[...] / total[:, :1]).astype(jnp.bfloat16)
        for member in range(group):
            heads_buf[part_no * group + member] = jnp.dot(
                attended[member * tok_rows : (member + 1) * tok_rows],
                value_up_ref[part_no * group + member],
                preferred_element_type=jnp.float32,
            ).astype(jnp.bfloat16)

    joined = jnp.concatenate([heads_buf[head] for head in range(heads)], axis=1)
    out_ref[...] = jnp.dot(
        joined, out_proj_ref[...], preferred_element_type=jnp.float32
    ).astype(out_ref.dtype)


def attend_rows(nope, rope, keys, key_up, value_up, out_proj, first, first_token):
    heads, tok_rows = nope.shape[0], nope.shape[1]
    key_tile = 512 if keys.shape[0] % 512 == 0 else 128
    width = keys.shape[1]
    span = jnp.stack(
        [
            jnp.min(first) // key_tile,
            (first_token + tok_rows + key_tile - 1) // key_tile,
            first_token,
        ]
    ).astype(jnp.int32)
    vmem = pl.BlockSpec(memory_space=pltpu.VMEM)
    rows = 4 * tok_rows
    return pl.pallas_call(
        functools.partial(attend_kernel, key_tile),
        out_shape=jax.ShapeDtypeStruct((tok_rows, out_proj.shape[1]), jnp.bfloat16),
        in_specs=[pl.BlockSpec(memory_space=pltpu.SMEM)] + [vmem] * 7,
        out_specs=vmem,
        scratch_shapes=[
            pltpu.VMEM((heads * tok_rows, width), jnp.bfloat16),
            pltpu.VMEM((rows, KV_RANK), jnp.float32),
            pltpu.VMEM((rows, 128), jnp.float32),
            pltpu.VMEM((rows, 128), jnp.float32),
            pltpu.VMEM((heads, tok_rows, V_HEAD), jnp.bfloat16),
        ],
        compiler_params=pltpu.CompilerParams(vmem_limit_bytes=40 * 1024 * 1024),
    )(span, first[:, None], nope, rope, keys, key_up, value_up, out_proj)


def body(
    hidden,
    queries,
    req_len,
    req_offset,
    expert_ids,
    decode_slot,
    attn_gain,
    kv_down,
    kv_gain,
    key_up,
    value_up,
    out_proj,
    ffn_gain,
    router,
    expert_gate_up,
    expert_down,
):
    head_count = lax.axis_size("head")
    seq_place = lax.axis_index("seq")
    head_place = lax.axis_index("head")
    tok_rows = hidden.shape[0]
    heads_here = key_up.shape[0]
    my_index = seq_place * tok_rows + jnp.arange(tok_rows, dtype=jnp.int32)
    my_request = request_of(req_len, my_index)
    my_turn = angles(position_of(req_len, req_offset, my_index), ROPE)
    normed = rms_rows(hidden, attn_gain).astype(jnp.bfloat16)
    head_view = queries.reshape(tok_rows, heads_here, NOPE + ROPE)
    query_rope = rotate(head_view[:, :, NOPE:], my_turn[:, None, :]).astype(jnp.bfloat16)
    query_latent = jnp.einsum(
        "thn,hnc->thc", head_view[:, :, :NOPE], key_up, preferred_element_type=jnp.float32
    ).astype(jnp.bfloat16)
    query_rows = tok_rows * heads_here
    flat_latent = query_latent.reshape(query_rows, KV_RANK)
    flat_rope = query_rope.reshape(query_rows, ROPE)
    row_token = jnp.repeat(my_index, heads_here)
    row_request = jnp.repeat(my_request, heads_here)
    score_scale = 1.0 / math.sqrt(NOPE + ROPE)
    my_device = seq_place * head_count + head_place
    slot_ids = my_device * DEC_SLOTS + jnp.arange(DEC_SLOTS, dtype=jnp.int32)
    block_ids = jnp.arange(decode_slot.shape[0], dtype=jnp.int32)
    slot_match = decode_slot[None, :] == slot_ids[:, None]
    source_block = jnp.sum(jnp.where(slot_match, block_ids[None, :], 0), axis=1)
    slot_filled = jnp.any(slot_match, axis=1)
    kv_full = jnp.dot(normed, kv_down, preferred_element_type=jnp.float32)
    latent = rms_rows(kv_full[:, :KV_RANK], kv_gain).astype(jnp.bfloat16)
    key_rope = rotate(kv_full[:, KV_RANK:], my_turn).astype(jnp.bfloat16)
    run_peak = jnp.full((query_rows,), MASKED, jnp.float32)
    run_total = jnp.zeros((query_rows,), jnp.float32)
    run_acc = jnp.zeros((query_rows, KV_RANK), jnp.float32)
    expert_count = router.shape[1]
    expert_axis = jnp.arange(expert_count, dtype=jnp.int32)
    seq_count = lax.axis_size("seq")
    fast = seq_count % 4 == 0 and seq_count <= 16 and head_count == 2 and expert_count <= 64
    if fast:
        route_mask = jnp.any(expert_ids[:, :, None] == expert_axis[None, None, :], axis=1)
        payload = jnp.concatenate([latent, key_rope, route_mask.astype(jnp.bfloat16)], axis=1)
        payload = jnp.pad(payload, ((0, 0), (0, -payload.shape[1] % 128)))
        gathered = gather_rows(payload, seq_count)
        all_masks = gathered[:, KV_RANK + ROPE : KV_RANK + ROPE + expert_count]
        by_head = jnp.swapaxes(head_view, 0, 1)
        rope_pad = gathered.shape[1] - KV_RANK - ROPE
        by_head_rope = jnp.pad(jnp.swapaxes(query_rope, 0, 1), ((0, 0), (0, 0), (0, rope_pad)))
        req_ends = running(req_len)
        member = my_request[:, None] == jnp.arange(req_len.shape[0])[None, :]
        first = jnp.sum(jnp.where(member, (req_ends - req_len)[None, :], 0), axis=1)
        attn_part = attend_rows(
            by_head[:, :, :NOPE],
            by_head_rope,
            gathered,
            key_up,
            value_up,
            out_proj,
            first,
            seq_place * tok_rows,
        )
        source_row = source_block[:, None] * BLOCK + jnp.arange(BLOCK, dtype=jnp.int32)[None, :]
        pick_rows = source_row[:, :, None] == jnp.arange(gathered.shape[0], dtype=jnp.int32)
        pick_rows = (pick_rows & slot_filled[:, None, None]).reshape(DEC_SLOTS * BLOCK, -1)
        slot_rows = jnp.dot(
            pick_rows.astype(jnp.bfloat16), gathered, preferred_element_type=jnp.float32
        ).astype(jnp.bfloat16)
        decode_latent = slot_rows[:, :KV_RANK].reshape(DEC_SLOTS, BLOCK, KV_RANK)
        decode_rope = slot_rows[:, KV_RANK : KV_RANK + ROPE].reshape(DEC_SLOTS, BLOCK * ROPE)
        output = expert_layer(
            hidden,
            attn_part,
            all_masks.reshape(seq_count, tok_rows, expert_count),
            ffn_gain,
            router,
            jnp.swapaxes(expert_gate_up[0], 1, 2),
            expert_down[0],
            seq_place,
            seq_count,
        )
        return (output, decode_latent, decode_rope)
    else:
        piece_latent = lax.all_gather(latent, "seq", axis=0, tiled=True)
        piece_rope = lax.all_gather(key_rope, "seq", axis=0, tiled=True)
    piece_rows = piece_latent.shape[0]
    block_width = key_width(piece_rows)

    def key_block(block_no, loop_state):
        peak_now, total_now, acc_now = loop_state
        offset_rows = block_no * block_width
        block_latent = lax.dynamic_slice_in_dim(piece_latent, offset_rows, block_width, 0)
        block_rope = lax.dynamic_slice_in_dim(piece_rope, offset_rows, block_width, 0)
        key_index = offset_rows + jnp.arange(block_width, dtype=jnp.int32)
        key_request = request_of(req_len, key_index)
        contract = (((1,), (1,)), ((), ()))
        scores = lax.dot_general(
            flat_latent, block_latent, contract, preferred_element_type=jnp.float32
        )
        scores = (
            scores
            + lax.dot_general(flat_rope, block_rope, contract, preferred_element_type=jnp.float32)
        ) * score_scale
        allowed = (key_index[None, :] <= row_token[:, None]) & (
            key_request[None, :] == row_request[:, None]
        )
        scores = jnp.where(allowed, scores, MASKED)
        new_peak = jnp.maximum(peak_now, jnp.max(scores, axis=1))
        exp_terms = jnp.where(allowed, jnp.exp(scores - new_peak[:, None]), 0.0)
        fade_factor = jnp.exp(peak_now - new_peak)
        total_now = total_now * fade_factor + jnp.sum(exp_terms, axis=1)
        acc_now = acc_now * fade_factor[:, None] + jnp.dot(
            exp_terms.astype(jnp.bfloat16), block_latent, preferred_element_type=jnp.float32
        )
        return (new_peak, total_now, acc_now)

    run_peak, run_total, run_acc = lax.fori_loop(
        0, piece_rows // block_width, key_block, (run_peak, run_total, run_acc)
    )
    block_count = piece_rows // BLOCK
    pick_matrix = (
        source_block[:, None] == jnp.arange(block_count, dtype=jnp.int32)[None, :]
    ) & slot_filled[:, None]
    pick_matrix = pick_matrix.astype(jnp.bfloat16)
    slot_latent = jnp.dot(
        pick_matrix,
        piece_latent.reshape(block_count, BLOCK * KV_RANK),
        preferred_element_type=jnp.float32,
    )
    slot_rope = jnp.dot(
        pick_matrix,
        piece_rope.reshape(block_count, BLOCK * ROPE),
        preferred_element_type=jnp.float32,
    )
    folded = (run_peak, run_total, run_acc, slot_latent, slot_rope)
    run_total = folded[1]
    run_acc = folded[2]
    slot_latent = folded[3]
    slot_rope = folded[4]
    attended = (
        (run_acc / run_total[:, None]).astype(jnp.bfloat16).reshape(tok_rows, heads_here, KV_RANK)
    )
    head_out = jnp.einsum(
        "thc,hcv->thv", attended, value_up, preferred_element_type=jnp.float32
    ).astype(jnp.bfloat16)
    attn_part = jnp.dot(
        head_out.reshape(tok_rows, heads_here * V_HEAD),
        out_proj,
        preferred_element_type=jnp.float32,
    )
    decode_latent = slot_latent.astype(jnp.bfloat16).reshape(DEC_SLOTS, BLOCK, KV_RANK)
    decode_rope = slot_rope.astype(jnp.bfloat16)
    mixed_rows = hidden.astype(jnp.float32) + lax.psum(
        attn_part.astype(jnp.bfloat16), "head"
    ).astype(jnp.float32)
    moe_in = rms_rows(mixed_rows, ffn_gain).astype(jnp.bfloat16)
    capacity = max(2, tok_rows * TOP * 4 // (3 * expert_count))
    gate_score = jax.nn.sigmoid(
        jnp.dot(moe_in.astype(jnp.float32), router, precision=lax.Precision.HIGHEST)
    )
    id_match = expert_ids[:, :, None] == expert_axis[None, None, :]
    chosen = jnp.sum(jnp.where(id_match, gate_score[:, None, :], 0.0), axis=2)
    gate_weight = ROUTE_SCALE * chosen / jnp.sum(chosen, axis=1, keepdims=True)
    flat_ids = expert_ids.reshape(-1)
    one_hot = (flat_ids[:, None] == expert_axis[None, :]).astype(jnp.int32)
    earlier = ranks(one_hot.T.astype(jnp.bfloat16)).T
    slot_rank = jnp.sum(earlier * one_hot, axis=1)
    flat_slot = flat_ids * capacity + slot_rank
    owner_token = jnp.repeat(jnp.arange(tok_rows, dtype=jnp.int32), TOP)
    slot_token = jnp.zeros((expert_count * capacity,), jnp.int32).at[flat_slot].set(owner_token)
    slot_used = jnp.zeros((expert_count * capacity,), jnp.bool_).at[flat_slot].set(True)
    send_rows = jnp.where(
        slot_used[:, None], moe_in[slot_token], jnp.zeros((), jnp.bfloat16)
    ).reshape(expert_count, capacity, D)
    gate_up_local = expert_gate_up[0]
    down_local = expert_down[0]
    quarter_cols = D // head_count
    arrived = lax.all_to_all(send_rows, "seq", split_axis=0, concat_axis=0, tiled=True)
    sources, item_count, width_cols = arrived.shape
    flat_rows = arrived.reshape(sources * item_count, width_cols)
    gate_part = jnp.dot(flat_rows, gate_up_local[0], preferred_element_type=jnp.float32)
    up_part = jnp.dot(flat_rows, gate_up_local[1], preferred_element_type=jnp.float32)
    activated = (jax.nn.silu(gate_part) * up_part).astype(jnp.bfloat16)
    part_out = (
        jnp.dot(activated, down_local, preferred_element_type=jnp.float32)
        .astype(jnp.bfloat16)
        .reshape(sources, item_count, width_cols)
    )
    returned = lax.all_to_all(part_out, "seq", split_axis=0, concat_axis=0, tiled=True)
    back_cols = returned.shape[2]
    picked = returned.reshape(expert_count * capacity, back_cols)[flat_slot].reshape(
        tok_rows, TOP, back_cols
    )
    weighted = jnp.sum(picked.astype(jnp.float32) * gate_weight[:, :, None], axis=1)
    moe_out = lax.psum_scatter(
        weighted.astype(jnp.bfloat16), "head", scatter_dimension=1, tiled=True
    ).astype(jnp.float32)
    residual_part = lax.dynamic_slice_in_dim(mixed_rows, head_place * quarter_cols, quarter_cols, 1)
    output = (residual_part + moe_out).astype(jnp.bfloat16)
    return (output, decode_latent, decode_rope)


def solution(mesh):
    placed = (
        P("seq", None),
        P("seq", "head"),
        P(),
        P(),
        P("seq", None),
        P(),
        P(),
        P(),
        P(),
        P("head", None, None),
        P("head", None, None),
        P("head", None),
        P(),
        P(),
        P("seq", None, None, "head"),
        P("seq", "head", None),
    )
    return jax.shard_map(
        body,
        mesh=mesh,
        in_specs=placed,
        out_specs=(P("seq", "head"), P(("seq", "head"), None, None), P(("seq", "head"), None)),
        check_vma=False,
    )
```

profile of v0, /device:TPU:0, one launch (start us, length us, event | category | flops | bytes accessed | tf_op | source)
XLA Modules:
  0.0 186.3 jit_solution(16101761353485887355)
XLA Ops:
  0.7 0.9 fusion.27
  1.6 0.7 sub.34
  2.3 0.8 compare_reduce_fusion.1
  3.1 0.8 fusion.26
  4.1 1.2 fusion
  5.5 0.8 select_reduce_fusion
  6.2 0.6 subtract_convert_fusion.1
  9.7 0.7 fusion.25
  10.4 1.3 reshape.164.gain_ref
  11.8 1.9 %fusion.10 = f32[128,576]{0,1:T(8,128)S(1)} fusion(bf16[2048,576]{0,1:T(8,128)(2,1)S(1)} %copy-done, bf16[128,2048]{1,0:T(8,128)(2,1)} %hidden_ref.1, f32[2048]{0:T(1024)} %param.22, f32[128]{0:T(128)S(1)} %add_rsqrt_fusion.1), kind=kOutput, calls=%fused_computation.23 | convolution fusion | flops 303038464 | bytes 3187200 | tf_op jit(solution)/shard_map/dot_general | solution.py:637
  14.3 0.7 copy.49
  15.1 0.7 copy.46
  15.8 0.2 copy.44
  16.1 0.7 copy-done.5
  16.8 1.2 copy.45
  18.1 1.0 copy.47
  19.1 1.4 fusion.7
  20.7 1.3 copy.53
  22.0 1.6 reduce-precision_convert_fusion.1
  23.6 1.4 pad_maximum_fusion.router_ref
  25.0 26.8 %shard_map.175 = bf16[16,2,64,640]{3,2,1,0:T(8,128)(2,1)S(1)} custom-call(bf16[2,64,640]{2,1,0:T(8,128)(2,1)S(1)} %bitcast.22), custom_call_target="tpu_custom_call" | custom-call | tf_op jit(solution)/shard_map/pallas_call | solution.py:209
  51.8 5.6 %shard_map.176.attn_ref = bf16[128,2048]{1,0:T(8,128)(2,1)S(1)} custom-call(s32[3]{0:T(128)S(1)} %pad_add_fusion.span_ref, s32[128,1]{1,0:T(8,128)S(1)} %copy.52.first_ref, bf16[8,128,128]{2,1,0:T(8,128)(2,1)S(1)} %slice.42.nope_ref, bf16[8,128,128]{2,1,0:T(8,128)(2,1)S(1)} %pad.16.rope_ref, bf16[2048,640]{1,0:T(8,128)(2,1)S(1)} %bitcast.19, ...), custom_call_target="tpu_custom_call" | custom-call | tf_op jit(solution)/shard_map/pallas_call | solution.py:577
  57.5 0.6 convolution_convert_fusion
  58.3 0.5 compare_reduce_fusion
  58.9 0.4 dynamic-slice_reduce_fusion
  59.4 1.1 fusion.12.chosen_ref
  60.5 0.6 slice.49
  61.1 0.7 reshape.167
  61.8 0.8 fusion.18.pick_ref
  62.6 1.4 fusion.5.place_ref
  64.0 120.6 %shard_map.177 = bf16[128,1024]{1,0:T(8,128)(2,1)} custom-call(bf16[128,2048]{1,0:T(8,128)(2,1)} %hidden_ref.1, bf16[128,2048]{1,0:T(8,128)(2,1)} %copy-done.2, f32[2,1024]{1,0:T(2,128)} %reshape.164.gain_ref, bf16[16,64,128]{2,1,0:T(8,128)(2,1)} %fusion.18.pick_ref, bf16[16,128,64]{2,1,0:T(8,128)(2,1)} %fusion.5.place_ref, ...), custom_call_target="tpu_custom_call" | custom-call | tf_op jit(solution)/shard_map/pallas_call | solution.py:453
  184.6 1.7 copy.56
  (45 shorter events, 1.9 us)
Async XLA Ops:
  0.6 11.2 %copy-start = (bf16[2048,576]{0,1:T(8,128)(2,1)S(1)}, bf16[2048,576]{0,1:T(8,128)(2,1)}, u32[]{:S(2)}) copy-start(bf16[2048,576]{0,1:T(8,128)(2,1)} %param.23) | copy-start | bytes 7077892
  0.6 13.3 %copy-start.8 = (f32[512]{0:T(512)S(1)}, f32[512]{0:T(512)}, u32[]{:S(2)}) copy-start(f32[512]{0:T(512)} %param.24) | copy-start | bytes 6148
  5.3 10.5 %copy-start.6 = (bf16[128,1536]{1,0:T(8,128)(2,1)S(1)}, bf16[128,1536]{1,0:T(8,128)(2,1)}, u32[]{:S(2)}) copy-start(bf16[128,1536]{1,0:T(8,128)(2,1)} %param.17) | copy-start | bytes 1179652
  16.0 0.7 copy-start.5
  19.1 1.6 copy-start.7
  22.0 29.8 %copy-start.4 = (bf16[8,512,128]{2,1,0:T(8,128)(2,1)S(1)}, bf16[8,512,128]{2,1,0:T(8,128)(2,1)}, u32[]{:S(2)}) copy-start(bf16[8,512,128]{2,1,0:T(8,128)(2,1)} %value_up_ref.1) | copy-start | bytes 3145732
  23.6 28.2 %copy-start.1 = (bf16[1024,2048]{1,0:T(8,128)(2,1)S(1)}, bf16[1024,2048]{1,0:T(8,128)(2,1)}, u32[]{:S(2)}) copy-start(bf16[1024,2048]{1,0:T(8,128)(2,1)} %out_proj_ref.1) | copy-start | bytes 12582916
  23.6 28.2 %copy-start.3 = (bf16[8,128,512]{2,1,0:T(8,128)(2,1)S(1)}, bf16[8,128,512]{2,1,0:T(8,128)(2,1)}, u32[]{:S(2)}) copy-start(bf16[8,128,512]{2,1,0:T(8,128)(2,1)} %key_up_ref.1) | copy-start | bytes 3145732
  57.5 3.0 %copy-start.2 = (bf16[128,2048]{1,0:T(8,128)(2,1)}, bf16[128,2048]{1,0:T(8,128)(2,1)S(1)}, u32[]{:S(2)}) copy-start(bf16[128,2048]{1,0:T(8,128)(2,1)S(1)} %shard_map.176.attn_ref) | copy-start | bytes 1572868
where the time goes:
time: 186 us
  Pallas kernels  153 us (82%)
  other arithmetic  14.4 us (8%)
  local copies, waits for them, and re-layouts  11.5 us (6%)
  matrix products  3.74 us (2%)
  between operations  3.51 us (2%)
    pallas_call x1, Pallas kernels, expert_layer(): pl.pallas_call(functools.partial(expert_kernel, nz), out_shape=jax.ShapeD...  121 us
    pallas_call x1, Pallas kernels, gather_rows(): pl.pallas_call(functools.partial(gather_kernel, nz), out_shape=jax.ShapeD...  26.8 us
    pallas_call x1, Pallas kernels, attend_rows(): pl.pallas_call(functools.partial(attend_kernel, key_tile), out_shape=jax....  5.65 us
    unnamed x22, local copies, waits for them, and re-layouts  4.17 us

commit v1 on v0

--- a/solution.py
+++ b/solution.py
@@ -219,14 +219,31 @@
     return out.reshape(seq_count * tok_rows, width)
 
 
+def line_place(line, s):
+    return line * 4 + lax.rem(s, 4)
+
+
+def across(s, step):
+    if step & 1:
+        s = flip(s, 1)
+    if step & 2:
+        s = flip(s, 2)
+    return s
+
+
+def turn_line(z, k):
+    upper = lax.div(z, 2)
+    near = z + upper * (3 - 2 * z)
+    late = lax.div(k, 2)
+    line = late * k + (1 - late) * (near + k * (1 - 2 * near))
+    return line + upper * (3 - 2 * line)
+
+
 def expert_kernel(
-    nz,
     hidden_ref,
     attn_ref,
     gain_ref,
-    pick_ref,
-    place_ref,
-    chosen_ref,
+    tail_ref,
     router_ref,
     gate_up_hbm,
     down_hbm,
@@ -234,257 +251,361 @@
     attn_in,
     mixed,
     x_buf,
-    part,
-    sib_buf,
-    t3_buf,
-    t2_buf,
-    t1_buf,
+    stage,
+    rows_in,
+    res,
+    sib_in,
+    ret_in,
+    z_out,
+    z_in,
+    pick_buf,
+    place_buf,
+    chosen_buf,
+    router_buf,
     gate_up,
     down,
-    rows_buf,
-    act_buf,
-    res_buf,
     load_sem,
     attn_sem,
-    e0_send,
-    e0_recv,
-    e3_send,
-    e3_recv,
-    e2_send,
-    e2_recv,
-    e1_send,
-    e1_recv,
-    *sems,
+    up_send,
+    up_recv,
+    down_send,
+    down_recv,
+    go_send,
+    go_recv,
+    share_send,
+    share_recv,
+    part_send,
+    part_recv,
+    ret_send,
+    ret_recv,
+    home_send,
+    home_recv,
 ):
     s, h = lax.axis_index("seq"), lax.axis_index("head")
+    z, c = lax.div(s, 4), lax.rem(s, 4)
     cols = hidden_ref.shape[1]
     half = cols // 2
-    slots = pick_ref.shape[1]
+    slots = stage.shape[2]
+    tok_rows = hidden_ref.shape[0]
+    expert_count = router_ref.shape[0]
+    sibling = (s, 1 - h)
     loads = [
         pltpu.make_async_copy(gate_up_hbm, gate_up, load_sem.at[0]),
         pltpu.make_async_copy(down_hbm, down, load_sem.at[1]),
     ]
     for load in loads:
         load.start()
-    meet(s, h, nz)
-    swap = pltpu.make_async_remote_copy(
-        src_ref=attn_ref,
-        dst_ref=attn_in,
-        send_sem=attn_sem.at[0],
-        recv_sem=attn_sem.at[1],
-        device_id=(s, 1 - h),
-        device_id_type=MESH,
-    )
-    swap.start()
-    swap.wait_recv()
-    total = hidden_ref[...].astype(jnp.float32) + (
-        attn_ref[...].astype(jnp.float32) + attn_in[...].astype(jnp.float32)
-    )
-    mixed[0] = total[:, :half]
-    mixed[1] = total[:, half:]
-    inverse = lax.rsqrt(jnp.mean(total * total, axis=1, keepdims=True) + EPSILON)
-    x_buf[h, s] = (mixed[h] * inverse * gain_ref[h][None, :]).astype(jnp.bfloat16)
-    spread = Spread(x_buf, s, h, nz, sems)
-    spread.send_all()
-    spread.pass_on(0)
-    for load in loads:
-        load.wait()
-
-    def remote(src, dst, send, recv, index, device):
+
+    def remote(src, dst, send, recv, device):
         return pltpu.make_async_remote_copy(
             src_ref=src,
             dst_ref=dst,
-            send_sem=send.at[index],
-            recv_sem=recv.at[index],
+            send_sem=send,
+            recv_sem=recv,
             device_id=device,
             device_id_type=MESH,
         )
 
-    sibling = (s, 1 - h)
-    partner2 = (flip(s, 2 - h), h)
-    partner3 = (flip(s, 1 + h), h)
-
-    def line_of(back):
-        return lax.rem(lax.div(s, 4) - back + nz, nz)
-
-    def give0(back):
-        base = pl.ds(line_of(back) * 4, 4)
-        return remote(part.at[1 - h, base], sib_buf.at[base], e0_send, e0_recv, back, sibling)
-
-    def give3(back, side):
-        block = place_of(s, h, nz, back, 2 + side)
-        index = 2 * back + side
-        return remote(part.at[h, block], t3_buf.at[index], e3_send, e3_recv, index, partner3)
-
-    def give2(back):
-        block = place_of(s, h, nz, back, 1)
-        return remote(part.at[h, block], t2_buf.at[back], e2_send, e2_recv, back, partner2)
-
-    def give1(back):
-        block = place_of(s, h, nz, back, 0)
-        return remote(part.at[h, block], t1_buf.at[back], e1_send, e1_recv, back, (block, h))
-
-    def add(block, other):
-        part[h, block] = (
-            part[h, block].astype(jnp.float32) + other.astype(jnp.float32)
-        ).astype(jnp.bfloat16)
-
-    def feed(back):
-        spread.sibling(back, False).wait_recv()
-        base = line_of(back) * 4
-        for c in range(4):
-            pick = pick_ref[base + c]
-            for side in range(2):
-                rows_buf[c * slots : (c + 1) * slots, side * half : (side + 1) * half] = jnp.dot(
-                    pick, x_buf[side, base + c], preferred_element_type=jnp.float32
-                ).astype(jnp.bfloat16)
-        rows = rows_buf[...]
-        logit = jnp.dot(rows, router_ref[...], preferred_element_type=jnp.float32)
-        width = logit.shape[1] // 3
-        logit = logit[:, :width] + (logit[:, width : 2 * width] + logit[:, 2 * width :])
+    barrier = pltpu.get_barrier_semaphore()
+    peers = [(line_place(lax.rem(z + back, 4), s), h) for back in range(1, 4)]
+    peers += [(across(s, step), h) for step in range(1, 4)] + [sibling]
+    for peer in peers:
+        pl.semaphore_signal(barrier, inc=1, device_id=peer, device_id_type=MESH)
+    pl.semaphore_wait(barrier, len(peers))
+
+    def up(t):
+        view = x_buf.at[z - t]
+        device = (line_place(lax.rem(z + 1, 4), s), h)
+        return remote(view, view, up_send.at[t], up_recv.at[t], device)
+
+    def up_in(t):
+        view = x_buf.at[z - t]
+        return remote(view, view, up_send.at[t - 1], up_recv.at[t - 1], sibling)
+
+    def low(t):
+        view = x_buf.at[z + t]
+        device = (line_place(lax.rem(z + 3, 4), s), h)
+        return remote(view, view, down_send.at[t], down_recv.at[t], device)
+
+    def low_in(t):
+        view = x_buf.at[z + t]
+        return remote(view, view, down_send.at[t - 1], down_recv.at[t - 1], sibling)
+
+    def go(k, step):
+        other = across(s, step)
+        index = 3 * k + step - 1
+        return remote(
+            stage.at[k, lax.rem(other, 4)],
+            rows_in.at[k, h, c],
+            go_send.at[index],
+            go_recv.at[index],
+            (other, h),
+        )
+
+    def go_in(k, step):
+        index = 3 * k + step - 1
+        view = rows_in.at[k, h, lax.rem(across(s, step), 4)]
+        return remote(view, view, go_send.at[index], go_recv.at[index], sibling)
+
+    def share(k):
+        view = rows_in.at[k, h]
+        return remote(view, view, share_send.at[k], share_recv.at[k], sibling)
+
+    def share_in(k):
+        view = rows_in.at[k, 1 - h]
+        return remote(view, view, share_send.at[k], share_recv.at[k], sibling)
+
+    def part(k):
+        return remote(res.at[k, 1 - h], sib_in.at[k], part_send.at[k], part_recv.at[k], sibling)
+
+    def ret(k, step):
+        other = across(s, step)
+        index = 3 * k + step - 1
+        return remote(
+            res.at[k, h, lax.rem(other, 4)],
+            ret_in.at[k, c],
+            ret_send.at[index],
+            ret_recv.at[index],
+            (other, h),
+        )
+
+    def ret_back(k, step):
+        index = 3 * k + step - 1
+        view = ret_in.at[k, lax.rem(across(s, step), 4)]
+        return remote(view, view, ret_send.at[index], ret_recv.at[index], sibling)
+
+    def home(k):
+        owner = (line_place(turn_line(z, k), s), h)
+        return remote(z_out.at[k], z_in.at[z], home_send.at[k], home_recv.at[z], owner)
+
+    def home_in(back):
+        line = lax.rem(z + back, 4)
+        return remote(z_in.at[line], z_in.at[line], home_send.at[0], home_recv.at[line], sibling)
+
+    swap = remote(attn_ref, attn_in, attn_sem.at[0], attn_sem.at[1], sibling)
+    swap.start()
+
+    def iota(shape, dim):
+        return lax.broadcasted_iota(jnp.int32, shape, dim)
+
+    bf16, f32 = jnp.bfloat16, jnp.float32
+    pair = (((1,), (1,)), ((), ()))
+    four = 4 * slots
+    lane = (tok_rows, 128)
+    before = (iota((tok_rows, tok_rows), 0) < iota((tok_rows, tok_rows), 1)).astype(bf16)
+    after = (iota((tok_rows, tok_rows), 0) > iota((tok_rows, tok_rows), 1)).astype(bf16)
+
+    def one_hot(flags):
+        return jnp.where(flags, 1.0, 0.0).astype(bf16)
+
+    def prepare(k):
+        line = turn_line(z, k)
+        tail = tail_ref[line * 4 + c]
+        shape = (four, 128)
+        named = one_hot(iota(shape, 1) == ROPE + 4 * z + lax.div(iota(shape, 0), slots))
+        slot = lax.rem(iota((four, tok_rows), 0), slots).astype(f32)
+        member = lax.dot_general(named, tail, pair, preferred_element_type=f32)
+        rank = jnp.dot(member.astype(bf16), before, preferred_element_type=f32)
+        pick_buf[k] = one_hot((rank == slot) & (member > 0.0))
+        shape = (128, four)
+        named = one_hot(iota(shape, 0) == ROPE + 4 * z + lax.div(iota(shape, 1), slots))
+        slot = lax.rem(iota((tok_rows, four), 1), slots).astype(f32)
+        member = jnp.dot(tail, named, preferred_element_type=f32)
+        rank = jnp.dot(after, member.astype(bf16), preferred_element_type=f32)
+        place_buf[k] = one_hot((rank == slot) & (member > 0.0))
+        named = one_hot(iota((slots, 128), 1) == ROPE + s)
+        slot = iota((slots, tok_rows), 0).astype(f32)
+        for block in range(4):
+            tail = tail_ref[line * 4 + block]
+            member = lax.dot_general(named, tail, pair, preferred_element_type=f32)
+            rank = jnp.dot(member.astype(bf16), before, preferred_element_type=f32)
+            mine = one_hot((rank == slot) & (member > 0.0))
+            chosen = jnp.dot(mine, tail, preferred_element_type=f32)
+            known = iota((slots, 128), 1)
+            known = (known >= ROPE) & (known < ROPE + expert_count)
+            chosen_buf[k, block * slots : (block + 1) * slots] = jnp.where(known, chosen, 0.0)
+
+    prepare(0)
+    router = router_ref[...]
+    high = router.astype(bf16)
+    rest = router - high.astype(f32)
+    middle = rest.astype(bf16)
+    last = (rest - middle.astype(f32)).astype(bf16)
+    top_pad = jnp.zeros((ROPE, cols), bf16)
+    low_pad = jnp.zeros((128 - ROPE - 3 * expert_count, cols), bf16)
+    router_buf[...] = jnp.concatenate([top_pad, high, middle, last, low_pad], axis=0)
+
+    swap.wait_recv()
+    total = hidden_ref[...].astype(f32) + (attn_ref[...].astype(f32) + attn_in[...].astype(f32))
+    inverse = lax.rsqrt(jnp.mean(total * total, axis=1, keepdims=True) + EPSILON)
+    gain = gain_ref[...]
+    mine = jnp.where(h == 0, total[:, :half], total[:, half:])
+    mixed[...] = mine
+    own_gain = jnp.where(h == 0, gain[:, :half], gain[:, half:])
+    x_buf[z] = (mine * inverse * own_gain).astype(bf16)
+
+    def ring(t):
+        @pl.when((t >= 1) & (t <= z))
+        def _():
+            up_in(t).wait_recv()
+
+        @pl.when((t <= z) & (z < 3))
+        def _():
+            up(t).start()
+
+        @pl.when((t >= 1) & (t <= 3 - z))
+        def _():
+            low_in(t).wait_recv()
+
+        @pl.when((t <= 3 - z) & (z > 0))
+        def _():
+            low(t).start()
+
+    def pick(k):
+        rows = jnp.dot(pick_buf[k], x_buf[turn_line(z, k)], preferred_element_type=f32)
+        stage[k] = rows.astype(bf16).reshape(4, slots, half)
+        for step in (3, 1, 2):
+            go(k, step).start()
+        rows_in[k, h, c] = stage[k, c]
+
+    def meet_rows(k):
+        for step in (1, 2, 3):
+            go_in(k, step).wait_recv()
+        share(k).start()
+
+    def work(k):
+        share_in(k).wait_recv()
+        rows = jnp.concatenate(
+            [rows_in[k, 0].reshape(four, half), rows_in[k, 1].reshape(four, half)], axis=1
+        )
+        logit = lax.dot_general(rows, router_buf[...], pair, preferred_element_type=f32)
+        logit = logit + (
+            pltpu.roll(logit, 128 - expert_count, 1) + pltpu.roll(logit, 128 - 2 * expert_count, 1)
+        )
         score = 1.0 / (1.0 + jnp.exp(-logit))
-        chosen = score * chosen_ref[pl.ds(base, 4)].reshape(4 * slots, width)
-        own = jnp.where(lax.broadcasted_iota(jnp.int32, chosen.shape, 1) == s, chosen, 0.0)
+        chosen = jnp.where(chosen_buf[k] > 0.0, score, 0.0)
+        own = jnp.where(iota(chosen.shape, 1) == ROPE + s, chosen, 0.0)
         own = jnp.sum(own, axis=1, keepdims=True)
         every = jnp.sum(chosen, axis=1, keepdims=True)
         weight = ROUTE_SCALE * own / jnp.where(every > 0.0, every, 1.0)
-        across = (((1,), (1,)), ((), ()))
-        gate = lax.dot_general(rows, gate_up[0], across, preferred_element_type=jnp.float32)
-        up = lax.dot_general(rows, gate_up[1], across, preferred_element_type=jnp.float32)
-        act_buf[...] = (gate / (1.0 + jnp.exp(-gate)) * up * weight).astype(jnp.bfloat16)
-        res_buf[...] = jnp.dot(
-            act_buf[...], down[...], preferred_element_type=jnp.float32
-        ).astype(jnp.bfloat16)
-        for c in range(4):
-            for side in range(2):
-                part[side, base + c] = jnp.dot(
-                    place_ref[base + c],
-                    res_buf[c * slots : (c + 1) * slots, side * half : (side + 1) * half],
-                    preferred_element_type=jnp.float32,
-                ).astype(jnp.bfloat16)
-        give0(back).start()
-
-    def fold0(back):
-        give0(back).wait_recv()
-        for turn in (2, 3, 1, 0):
-            block = place_of(s, h, nz, back, turn)
-            add(block, sib_buf[block])
-            if turn >= 2:
-                give3(back, turn - 2).start()
-
-    def fold3(back):
-        for side in (1, 0):
-            give3(back, side).wait_recv()
-            add(place_of(s, h, nz, back, side), t3_buf[2 * back + side])
-            if side:
-                give2(back).start()
-
-    def fold2(back):
-        give2(back).wait_recv()
-        add(place_of(s, h, nz, back, 0), t2_buf[back])
-
-        @pl.when(back > 0)
-        def _():
-            give1(back).start()
-
-    @pl.loop(0, nz + 3)
-    def _(step):
-        @pl.when(step < nz)
-        def _():
-            feed(step)
-
-        @pl.when(step < nz - 1)
-        def _():
-            spread.pass_on(step + 1)
-
-        @pl.when((step >= 3))
-        def _():
-            fold2(step - 3)
-
-        @pl.when((step >= 2) & (step < nz + 2))
-        def _():
-            fold3(step - 2)
-
-        @pl.when((step >= 1) & (step < nz + 1))
-        def _():
-            fold0(step - 1)
-
-    result = mixed[h] + part[h, s].astype(jnp.float32)
-    for back in range(1, nz):
-        give1(back).wait_recv()
-        result = result + t1_buf[back].astype(jnp.float32)
+        gate = lax.dot_general(rows, gate_up[0], pair, preferred_element_type=f32)
+        rise = lax.dot_general(rows, gate_up[1], pair, preferred_element_type=f32)
+        act = (gate / (1.0 + jnp.exp(-gate)) * rise * weight).astype(bf16)
+        out = jnp.dot(act, down[...], preferred_element_type=f32).astype(bf16)
+        res[k, 0] = out[:, :half].reshape(4, slots, half)
+        res[k, 1] = out[:, half:].reshape(4, slots, half)
+        part(k).start()
+
+    def send_back(k):
+        part(k).wait_recv()
+        res[k, h] = (res[k, h].astype(f32) + sib_in[k].astype(f32)).astype(bf16)
+        for step in (3, 1, 2):
+            ret(k, step).start()
+        ret_in[k, c] = res[k, h, c]
+
+    def place(k):
+        for step in (1, 2, 3):
+            ret_back(k, step).wait_recv()
+        return jnp.dot(place_buf[k], ret_in[k].reshape(four, half), preferred_element_type=f32)
+
+    @pl.loop(0, 6)
+    def _(t):
+        @pl.when(t >= 3)
+        def _():
+            send_back(t - 2)
+
+        @pl.when(t <= 3)
+        def _():
+            ring(t)
+            pick(t)
+
+        @pl.when(t <= 2)
+        def _():
+            prepare(t + 1)
+
+        @pl.when(t == 1)
+        def _():
+            for load in loads:
+                load.wait()
+
+        @pl.when((t >= 1) & (t <= 4))
+        def _():
+            meet_rows(t - 1)
+            work(t - 1)
+
+    send_back(0)
+
+    @pl.loop(1, 4)
+    def _(k):
+        z_out[k] = place(k).astype(bf16)
+        home(k).start()
+
+    result = mixed[...] + place(0)
+    for back in (1, 2, 3):
+        home_in(back).wait_recv()
+        result = result + z_in[lax.rem(z + back, 4)].astype(f32)
     out_ref[...] = result.astype(out_ref.dtype)
     swap.wait_send()
-    spread.drain()
-    for back in range(nz):
-        give0(back).wait_send()
-        give3(back, 0).wait_send()
-        give3(back, 1).wait_send()
-        give2(back).wait_send()
-        if back:
-            give1(back).wait_send()
-
-
-def expert_layer(hidden, attn_part, masks, ffn_gain, router, gate_up, down, seq_place, seq_count):
+
+    @pl.loop(0, 4)
+    def _(k):
+        @pl.when((k <= z) & (z < 3))
+        def _():
+            up(k).wait_send()
+
+        @pl.when((k <= 3 - z) & (z > 0))
+        def _():
+            low(k).wait_send()
+
+        for step in (1, 2, 3):
+            go(k, step).wait_send()
+            ret(k, step).wait_send()
+        share(k).wait_send()
+        part(k).wait_send()
+
+        @pl.when(k > 0)
+        def _():
+            home(k).wait_send()
+
+
+def expert_layer(hidden, attn_part, tail, ffn_gain, router, gate_up, down):
     tok_rows, cols = hidden.shape
     half = cols // 2
-    nz = seq_count // 4
     expert_count = router.shape[1]
-    hidden_units = down.shape[0]
-    capacity = max(2, tok_rows * TOP * 4 // (3 * expert_count))
-    mine = lax.dynamic_index_in_dim(masks, seq_place, 2, keepdims=False)
-    rank = ranks(mine)
-    slot = jnp.arange(capacity, dtype=jnp.int32)
-    pick = (rank[:, None, :] == slot[None, :, None]) & (mine[:, None, :] > 0)
-    pick = pick.astype(jnp.bfloat16)
-    place = (rank[:, :, None] == slot[None, None, :]) & (mine[:, :, None] > 0)
-    place = place.astype(jnp.bfloat16)
-    wide_masks = jnp.pad(masks, ((0, 0), (0, 0), (0, 128 - expert_count)))
-    chosen = jnp.einsum("brt,bte->bre", pick, wide_masks, preferred_element_type=jnp.float32)
-    router = jnp.pad(router, ((0, 0), (0, 128 - expert_count)))
-    high = lax.reduce_precision(router, 8, 7)
-    middle = lax.reduce_precision(router - high, 8, 7)
-    low = router - high - middle
-    router3 = jnp.concatenate([high, middle, low], axis=1).astype(jnp.bfloat16)
+    slots = max(2, tok_rows * TOP * 4 // (3 * expert_count))
     vmem = pl.BlockSpec(memory_space=pltpu.VMEM)
     hbm = pl.BlockSpec(memory_space=pl.ANY)
     dma = pltpu.SemaphoreType.DMA
-    bf16 = jnp.bfloat16
+    bf16, f32 = jnp.bfloat16, jnp.float32
+    sizes = [2, 2] + [4] * 4 + [12] * 2 + [4] * 4 + [12] * 2 + [4] * 2
     return pl.pallas_call(
-        functools.partial(expert_kernel, nz),
+        expert_kernel,
         out_shape=jax.ShapeDtypeStruct((tok_rows, half), bf16),
-        in_specs=[vmem] * 7 + [hbm] * 2,
+        in_specs=[vmem] * 5 + [hbm] * 2,
         out_specs=vmem,
         scratch_shapes=[
             pltpu.VMEM((tok_rows, cols), bf16),
-            pltpu.VMEM((2, tok_rows, half), jnp.float32),
-            pltpu.VMEM((2, seq_count, tok_rows, half), bf16),
-            pltpu.VMEM((2, seq_count, tok_rows, half), bf16),
-            pltpu.VMEM((seq_count, tok_rows, half), bf16),
-            pltpu.VMEM((2 * nz, tok_rows, half), bf16),
-            pltpu.VMEM((nz, tok_rows, half), bf16),
-            pltpu.VMEM((nz, tok_rows, half), bf16),
+            pltpu.VMEM((tok_rows, half), f32),
+            pltpu.VMEM((4, tok_rows, half), bf16),
+            pltpu.VMEM((4, 4, slots, half), bf16),
+            pltpu.VMEM((4, 2, 4, slots, half), bf16),
+            pltpu.VMEM((4, 2, 4, slots, half), bf16),
+            pltpu.VMEM((4, 4, slots, half), bf16),
+            pltpu.VMEM((4, 4, slots, half), bf16),
+            pltpu.VMEM((4, tok_rows, half), bf16),
+            pltpu.VMEM((4, tok_rows, half), bf16),
+            pltpu.VMEM((4, 4 * slots, tok_rows), bf16),
+            pltpu.VMEM((4, tok_rows, 4 * slots), bf16),
+            pltpu.VMEM((4, 4 * slots, 128), f32),
+            pltpu.VMEM((128, cols), bf16),
             pltpu.VMEM(gate_up.shape, bf16),
             pltpu.VMEM(down.shape, bf16),
-            pltpu.VMEM((4 * capacity, cols), bf16),
-            pltpu.VMEM((4 * capacity, hidden_units), bf16),
-            pltpu.VMEM((4 * capacity, cols), bf16),
-            dma((2,)),
-            dma((2,)),
-            dma((nz,)),
-            dma((nz,)),
-            dma((2 * nz,)),
-            dma((2 * nz,)),
-            dma((nz,)),
-            dma((nz,)),
-            dma((nz,)),
-            dma((nz,)),
         ]
-        + spread_sems(nz),
+        + [dma((size,)) for size in sizes],
         compiler_params=pltpu.CompilerParams(
             collective_id=1, has_side_effects=True, vmem_limit_bytes=56 * 1024 * 1024
         ),
-    )(hidden, attn_part, ffn_gain.reshape(2, half), pick, place, chosen, router3, gate_up, down)
+    )(hidden, attn_part, ffn_gain[None, :], tail, router.T, gate_up, down)
 
 
 def attend_kernel(
@@ -643,13 +764,12 @@
     expert_count = router.shape[1]
     expert_axis = jnp.arange(expert_count, dtype=jnp.int32)
     seq_count = lax.axis_size("seq")
-    fast = seq_count % 4 == 0 and seq_count <= 16 and head_count == 2 and expert_count <= 64
+    fast = seq_count == 16 and head_count == 2 and expert_count == 16
     if fast:
         route_mask = jnp.any(expert_ids[:, :, None] == expert_axis[None, None, :], axis=1)
         payload = jnp.concatenate([latent, key_rope, route_mask.astype(jnp.bfloat16)], axis=1)
         payload = jnp.pad(payload, ((0, 0), (0, -payload.shape[1] % 128)))
         gathered = gather_rows(payload, seq_count)
-        all_masks = gathered[:, KV_RANK + ROPE : KV_RANK + ROPE + expert_count]
         by_head = jnp.swapaxes(head_view, 0, 1)
         rope_pad = gathered.shape[1] - KV_RANK - ROPE
         by_head_rope = jnp.pad(jnp.swapaxes(query_rope, 0, 1), ((0, 0), (0, 0), (0, rope_pad)))
@@ -674,16 +794,15 @@
         ).astype(jnp.bfloat16)
         decode_latent = slot_rows[:, :KV_RANK].reshape(DEC_SLOTS, BLOCK, KV_RANK)
         decode_rope = slot_rows[:, KV_RANK : KV_RANK + ROPE].reshape(DEC_SLOTS, BLOCK * ROPE)
+        tail = gathered[:, KV_RANK : KV_RANK + 128].reshape(seq_count, tok_rows, 128)
         output = expert_layer(
             hidden,
             attn_part,
-            all_masks.reshape(seq_count, tok_rows, expert_count),
+            tail,
             ffn_gain,
             router,
             jnp.swapaxes(expert_gate_up[0], 1, 2),
             expert_down[0],
-            seq_place,
-            seq_count,
         )
         return (output, decode_latent, decode_rope)
     else:

time: 186 us -> 141 us (0.76)
  Pallas kernels: 153 us -> 113 us
  other arithmetic: 14.4 us -> 9.6 us
    pallas_call x1, Pallas kernels: 121 us -> 80.9 us  [expert_layer(): pl.pallas_call(expert_kernel, out_shape=jax.ShapeDtypeStruct((tok_rows, h...]
    convert_element_type x2 -> x0, other arithmetic: 2.19 us -> none  [the longest x1 1.39 us: expert_layer(): place = place.astype(jnp.bfloat16)]
    unnamed x22 -> x21, local copies, waits for them, and re-layouts: 4.17 us -> 3.15 us
where the time goes in v1:
time: 141 us
  Pallas kernels  113 us (80%)
  local copies, waits for them, and re-layouts  11.9 us (8%)
  other arithmetic  9.6 us (7%)
  between operations  3.46 us (2%)
  matrix products  2.51 us (2%)
    pallas_call x1, Pallas kernels, expert_layer(): pl.pallas_call(expert_kernel, out_shape=jax.ShapeDtypeStruct((tok_rows, h...  80.9 us
    pallas_call x1, Pallas kernels, gather_rows(): pl.pallas_call(functools.partial(gather_kernel, nz), out_shape=jax.ShapeD...  26.8 us
    pallas_call x1, Pallas kernels, attend_rows(): pl.pallas_call(functools.partial(attend_kernel, key_tile), out_shape=jax....  5.49 us
    unnamed x21, local copies, waits for them, and re-layouts  3.15 us

profile of v1, /device:TPU:0, one launch (start us, length us, event | category | flops | bytes accessed | tf_op | source)
XLA Modules:
  0.0 140.7 jit_solution(984993249152429904)
XLA Ops:
  0.7 0.9 fusion.17
  1.6 0.7 sub.27
  2.3 0.8 compare_reduce_fusion
  3.1 0.8 fusion.16
  4.1 1.2 fusion
  5.4 0.8 select_reduce_fusion
  6.2 0.6 subtract_convert_fusion.1
  9.7 0.7 fusion.15
  10.4 0.1 copy.49.first_ref
  10.5 1.9 %fusion.7 = f32[128,576]{0,1:T(8,128)S(1)} fusion(bf16[2048,576]{0,1:T(8,128)(2,1)S(1)} %copy-done, bf16[128,2048]{1,0:T(8,128)(2,1)} %hidden_ref.1, f32[2048]{0:T(1024)} %param.22, f32[128]{0:T(128)S(1)} %add_rsqrt_fusion.1), kind=kOutput, calls=%fused_computation.12 | convolution fusion | flops 303038464 | bytes 3187200 | tf_op jit(solution)/shard_map/dot_general | solution.py:758
  12.5 0.1 subtract_convert_fusion
  12.7 0.1 multiply_convert_fusion
  12.8 0.2 copy.50
  13.0 0.7 pad.9.clone
  13.7 0.1 copy.46
  13.8 0.7 copy.43
  14.5 0.2 copy.41
  14.8 0.7 slice_convert_fusion
  15.4 1.0 copy.42
  16.5 1.8 %slice.42.nope_ref = bf16[8,128,128]{2,1,0:T(8,128)(2,1)} slice(bf16[8,128,192]{2,1,0:T(8,128)(2,1)} %bitcast.27), slice={[0:8], [0:128], [0:128]} | slice | bytes 524288 | tf_op jit(solution)/shard_map/slice | solution.py:780
  18.2 1.9 %copy.44 = f32[128,8,32]{2,0,1:T(8,128)} copy(f32[128,8,32]{0,2,1:T(8,128)} %slice_convert_fusion) | data formatting | bytes 262144 | tf_op jit(solution)/shard_map/convert_element_type | solution.py:42
  20.1 1.5 %fusion.4 = (bf16[128,8,32]{2,0,1:T(8,128)(2,1)S(1)}, bf16[128,8,32]{2,0,1:T(8,128)(2,1)S(1)}) fusion(f32[128,8,32]{2,0,1:T(8,128)} %copy.44, f32[128,32]{1,0:T(8,128)S(1)} %copy.46, f32[128,32]{1,0:T(8,128)} %copy.43, bf16[128,8,192]{2,0,1:T(8,128)(2,1)} %copy.42), kind=kLoop, calls=%fused_computation.9 | loop fusion | flops 294912 | bytes 360448 | tf_op jit(solution)/shard_map/convert.2
  21.7 0.1 maximum_bitcast_fusion
  21.9 1.1 copy-done.6
  23.0 26.8 %shard_map.175 = bf16[16,2,64,640]{3,2,1,0:T(8,128)(2,1)S(1)} custom-call(bf16[2,64,640]{2,1,0:T(8,128)(2,1)S(1)} %bitcast.23), custom_call_target="tpu_custom_call" | custom-call | tf_op jit(solution)/shard_map/pallas_call | solution.py:209
  49.8 5.5 %shard_map.176.attn_ref = bf16[128,2048]{1,0:T(8,128)(2,1)S(1)} custom-call(s32[3]{0:T(128)S(1)} %pad_add_fusion.span_ref, s32[128,1]{1,0:T(8,128)S(1)} %copy.49.first_ref, bf16[8,128,128]{2,1,0:T(8,128)(2,1)S(1)} %copy-done.5, bf16[8,128,128]{2,1,0:T(8,128)(2,1)S(1)} %pad.8.rope_ref, bf16[2048,640]{1,0:T(8,128)(2,1)S(1)} %bitcast.20, ...), custom_call_target="tpu_custom_call" | custom-call | tf_op jit(solution)/shard_map/pallas_call | solution.py:698
  55.4 0.6 convolution_convert_fusion
  56.0 0.8 slice.48
  56.8 80.9 %shard_map.177 = bf16[128,1024]{1,0:T(8,128)(2,1)} custom-call(bf16[128,2048]{1,0:T(8,128)(2,1)} %hidden_ref.1, bf16[128,2048]{1,0:T(8,128)(2,1)} %copy-done.2, f32[1,2048]{1,0:T(1,128)} %bitcast.32, bf16[16,128,128]{2,1,0:T(8,128)(2,1)} %bitcast.26, f32[16,2048]{1,0:T(8,128)} %bitcast.30, bf16[2,704,2048]{2,1,0:T(8,128)(2,1)} %bitcast.24, ...), custom_call_target="tpu_custom_call" | custom-call | tf_op jit(solution)/shard_map/pallas_call | solution.py:581
  137.7 0.6 slice.49
  138.4 0.7 reshape.153
  139.0 1.7 %copy.52 = bf16[128,1024]{1,0:T(8,128)(2,1)} copy(bf16[128,1024]{1,0:T(8,128)(2,1)} %shard_map.177) | data formatting | bytes 524288
  (34 shorter events, 0.7 us)
Async XLA Ops:
  0.6 9.9 %copy-start = (bf16[2048,576]{0,1:T(8,128)(2,1)S(1)}, bf16[2048,576]{0,1:T(8,128)(2,1)}, u32[]{:S(2)}) copy-start(bf16[2048,576]{0,1:T(8,128)(2,1)} %param.23) | copy-start | bytes 7077892
  0.6 12.0 %copy-start.8 = (f32[512]{0:T(512)S(1)}, f32[512]{0:T(512)}, u32[]{:S(2)}) copy-start(f32[512]{0:T(512)} %param.24) | copy-start | bytes 6148
  5.3 9.2 %copy-start.7 = (bf16[128,1536]{1,0:T(8,128)(2,1)S(1)}, bf16[128,1536]{1,0:T(8,128)(2,1)}, u32[]{:S(2)}) copy-start(bf16[128,1536]{1,0:T(8,128)(2,1)} %param.17) | copy-start | bytes 1179652
  16.5 33.3 %copy-start.4 = (bf16[8,512,128]{2,1,0:T(8,128)(2,1)S(1)}, bf16[8,512,128]{2,1,0:T(8,128)(2,1)}, u32[]{:S(2)}) copy-start(bf16[8,512,128]{2,1,0:T(8,128)(2,1)} %value_up_ref.1) | copy-start | bytes 3145732
  20.1 29.7 %copy-start.1 = (bf16[1024,2048]{1,0:T(8,128)(2,1)S(1)}, bf16[1024,2048]{1,0:T(8,128)(2,1)}, u32[]{:S(2)}) copy-start(bf16[1024,2048]{1,0:T(8,128)(2,1)} %out_proj_ref.1) | copy-start | bytes 12582916
  20.1 29.7 %copy-start.3 = (bf16[8,128,512]{2,1,0:T(8,128)(2,1)S(1)}, bf16[8,128,512]{2,1,0:T(8,128)(2,1)}, u32[]{:S(2)}) copy-start(bf16[8,128,512]{2,1,0:T(8,128)(2,1)} %key_up_ref.1) | copy-start | bytes 3145732
  20.1 29.7 %copy-start.5 = (bf16[8,128,128]{2,1,0:T(8,128)(2,1)S(1)}, bf16[8,128,128]{2,1,0:T(8,128)(2,1)}, u32[]{:S(2)}) copy-start(bf16[8,128,128]{2,1,0:T(8,128)(2,1)} %slice.42.nope_ref) | copy-start | bytes 786436
  21.9 1.1 copy-start.6
  55.3 1.5 %copy-start.2 = (bf16[128,2048]{1,0:T(8,128)(2,1)}, bf16[128,2048]{1,0:T(8,128)(2,1)S(1)}, u32[]{:S(2)}) copy-start(bf16[128,2048]{1,0:T(8,128)(2,1)S(1)} %shard_map.176.attn_ref) | copy-start | bytes 1572868

commit v2 on v1

--- a/solution.py
+++ b/solution.py
@@ -3,6 +3,7 @@
 
 import jax
 import jax.numpy as jnp
+import numpy as np
 from jax import lax
 from jax.experimental import pallas as pl
 from jax.experimental.pallas import tpu as pltpu
@@ -90,133 +91,6 @@
 
 def flip(place, step):
     return place + step * (1 - 2 * lax.rem(lax.div(place, step), 2))
-
-
-def place_of(s, h, nz, back, turn):
-    line = lax.rem(lax.div(s, 4) - back + nz, nz)
-    block = line * 4 + lax.rem(s, 4)
-    if turn & 1:
-        block = flip(block, 2 - h)
-    if turn & 2:
-        block = flip(block, 1 + h)
-    return block
-
-
-def meet(s, h, nz):
-    barrier = pltpu.get_barrier_semaphore()
-    peers = [(place_of(s, h, nz, back, 0), h) for back in range(1, nz)]
-    peers += [(flip(s, 2 - h), h), (flip(s, 1 + h), h), (s, 1 - h)]
-    for peer in peers:
-        pl.semaphore_signal(barrier, inc=1, device_id=peer, device_id_type=MESH)
-    pl.semaphore_wait(barrier, len(peers))
-
-
-class Spread:
-    def __init__(self, buf, s, h, nz, sems, blocks_first=False):
-        self.blocks_first = blocks_first
-        self.buf, self.s, self.h, self.nz = buf, s, h, nz
-        self.sems = sems
-
-    def move(self, block, kind, index, device):
-        view = self.buf.at[block, self.h] if self.blocks_first else self.buf.at[self.h, block]
-        return pltpu.make_async_remote_copy(
-            src_ref=view,
-            dst_ref=view,
-            send_sem=self.sems[2 * kind].at[index],
-            recv_sem=self.sems[2 * kind + 1].at[index],
-            device_id=device,
-            device_id_type=MESH,
-        )
-
-    def block(self, back, turn):
-        return place_of(self.s, self.h, self.nz, back, turn)
-
-    def line(self, ahead):
-        device = (place_of(self.s, self.h, self.nz, self.nz - ahead, 0), self.h)
-        return self.move(self.block(0, 0), 0, ahead, device)
-
-    def line_in(self, back):
-        return self.move(self.block(back, 0), 0, back, (self.s, 1 - self.h))
-
-    def second(self, back, turn=0):
-        return self.move(self.block(back, turn), 1, back, (flip(self.s, 2 - self.h), self.h))
-
-    def third(self, back, side, turn=0):
-        device = (flip(self.s, 1 + self.h), self.h)
-        return self.move(self.block(back, turn + side), 2, 2 * back + side, device)
-
-    def sibling(self, back, mine):
-        half = self.h if mine else 1 - self.h
-        line = lax.rem(lax.div(self.s, 4) - back + self.nz, self.nz)
-        four = pl.ds(line * 4, 4)
-        view = self.buf.at[four, half] if self.blocks_first else self.buf.at[half, four]
-        return pltpu.make_async_remote_copy(
-            src_ref=view,
-            dst_ref=view,
-            send_sem=self.sems[6].at[back],
-            recv_sem=self.sems[7].at[back],
-            device_id=(self.s, 1 - self.h),
-            device_id_type=MESH,
-        )
-
-    def send_all(self):
-        for ahead in range(1, self.nz):
-            self.line(ahead).start()
-        for back in range(self.nz):
-            if back:
-                self.line_in(back).wait_recv()
-            self.third(back, 0).start()
-            self.second(back).start()
-            self.second(back, 1).wait_recv()
-            self.third(back, 1).start()
-
-    def pass_on(self, back):
-        for side in range(2):
-            self.third(back, side, 2).wait_recv()
-        self.sibling(back, True).start()
-
-    def drain(self):
-        for ahead in range(1, self.nz):
-            self.line(ahead).wait_send()
-        for back in range(self.nz):
-            self.second(back).wait_send()
-            self.third(back, 0).wait_send()
-            self.third(back, 1).wait_send()
-            self.sibling(back, True).wait_send()
-
-
-def spread_sems(nz):
-    dma = pltpu.SemaphoreType.DMA
-    return [dma((nz,)), dma((nz,)), dma((nz,)), dma((nz,)), dma((2 * nz,)), dma((2 * nz,)), dma((nz,)), dma((nz,))]
-
-
-def gather_kernel(nz, rows_ref, out_ref, *sems):
-    s, h = lax.axis_index("seq"), lax.axis_index("head")
-    out_ref[s, h] = rows_ref[h]
-    meet(s, h, nz)
-    spread = Spread(out_ref, s, h, nz, sems, True)
-    spread.send_all()
-    for back in range(nz):
-        spread.pass_on(back)
-    for back in range(nz):
-        spread.sibling(back, False).wait_recv()
-    spread.drain()
-
-
-def gather_rows(rows, seq_count):
-    tok_rows, width = rows.shape
-    nz = seq_count // 4
-    out = pl.pallas_call(
-        functools.partial(gather_kernel, nz),
-        out_shape=jax.ShapeDtypeStruct((seq_count, 2, tok_rows // 2, width), rows.dtype),
-        in_specs=[pl.BlockSpec(memory_space=pltpu.VMEM)],
-        out_specs=pl.BlockSpec(memory_space=pltpu.VMEM),
-        scratch_shapes=spread_sems(nz),
-        compiler_params=pltpu.CompilerParams(
-            collective_id=0, has_side_effects=True, vmem_limit_bytes=16 * 1024 * 1024
-        ),
-    )(rows.reshape(2, tok_rows // 2, width))
-    return out.reshape(seq_count * tok_rows, width)
 
 
 def line_place(line, s):
@@ -608,107 +482,350 @@
     )(hidden, attn_part, ffn_gain[None, :], tail, router.T, gate_up, down)
 
 
-def attend_kernel(
-    key_tile,
-    span_ref,
-    first_ref,
-    nope_ref,
-    rope_ref,
-    keys_ref,
-    key_up_ref,
-    value_up_ref,
-    out_proj_ref,
+def front_kernel(
+    req_len_ref,
+    req_offset_ref,
+    freq_ref,
+    hidden_ref,
+    gain_ref,
+    kv_ref,
+    kv_gain_ref,
+    ids_ref,
+    queries_hbm,
+    key_up_hbm,
+    value_up_hbm,
+    out_proj_hbm,
     out_ref,
+    attn_ref,
+    queries,
+    key_up,
+    value_up,
+    out_proj,
     query,
     acc,
     peak,
     total,
     heads_buf,
+    load_sem,
+    up_send,
+    up_recv,
+    down_send,
+    down_recv,
+    plane_send,
+    plane_recv,
+    share_send,
+    share_recv,
 ):
-    heads, tok_rows = nope_ref.shape[0], nope_ref.shape[1]
-    group = 4
-    group_rows = group * tok_rows
-    score_scale = 1.0 / math.sqrt(NOPE + ROPE)
-    contract = (((1,), (1,)), ((), ()))
+    s, h = lax.axis_index("seq"), lax.axis_index("head")
+    z, c = lax.div(s, 4), lax.rem(s, 4)
+    bf16, f32 = jnp.bfloat16, jnp.float32
+    pair = (((1,), (1,)), ((), ()))
+    tok_rows = hidden_ref.shape[0]
+    rows_half = tok_rows // 2
+    heads = key_up.shape[0]
+    part_heads = heads // 2
+    part_rows = part_heads * tok_rows
+    tile_keys = 4 * tok_rows
+    sibling = (s, 1 - h)
+    pairs = [(queries_hbm, queries), (key_up_hbm, key_up)]
+    pairs += [(value_up_hbm, value_up), (out_proj_hbm, out_proj)]
+    loads = [pltpu.make_async_copy(*both, load_sem.at[i]) for i, both in enumerate(pairs)]
+    for load in loads:
+        load.start()
+
+    barrier = pltpu.get_barrier_semaphore()
+    peers = [(line_place(lax.rem(z + back, 4), s), h) for back in (1, 3)]
+    peers += [(across(s, step), h) for step in range(1, 4)] + [sibling]
+    for peer in peers:
+        pl.semaphore_signal(barrier, inc=1, device_id=peer, device_id_type=MESH)
+
+    def iota(shape, dim):
+        return lax.broadcasted_iota(jnp.int32, shape, dim)
+
+    def remote(src, dst, send, recv, device):
+        return pltpu.make_async_remote_copy(
+            src_ref=src,
+            dst_ref=dst,
+            send_sem=send,
+            recv_sem=recv,
+            device_id=device,
+            device_id_type=MESH,
+        )
+
+    def up(t):
+        view = out_ref.at[(z - t) * 4 + c, h]
+        device = (line_place(lax.rem(z + 1, 4), s), h)
+        return remote(view, view, up_send.at[t], up_recv.at[t], device)
+
+    def up_in(t):
+        view = out_ref.at[(z - t) * 4 + c, h]
+        return remote(view, view, up_send.at[t - 1], up_recv.at[t - 1], sibling)
+
+    def low(t):
+        view = out_ref.at[(z + t) * 4 + c, h]
+        device = (line_place(lax.rem(z + 3, 4), s), h)
+        return remote(view, view, down_send.at[t], down_recv.at[t], device)
+
+    def low_in(t):
+        view = out_ref.at[(z + t) * 4 + c, h]
+        return remote(view, view, down_send.at[t - 1], down_recv.at[t - 1], sibling)
+
+    def line_of(k):
+        return jnp.where(k <= z, z - k, k)
+
+    def plane(k, step):
+        view = out_ref.at[line_of(k) * 4 + c, h]
+        index = 3 * k + step - 1
+        device = (across(s, step), h)
+        return remote(view, view, plane_send.at[index], plane_recv.at[index], device)
+
+    def plane_in(k, step):
+        view = out_ref.at[line_of(k) * 4 + lax.rem(across(s, step), 4), h]
+        index = 3 * k + step - 1
+        return remote(view, view, plane_send.at[index], plane_recv.at[index], sibling)
+
+    def share(k):
+        view = out_ref.at[pl.ds(line_of(k) * 4, 4), h]
+        return remote(view, view, share_send.at[k], share_recv.at[k], sibling)
+
+    def share_in(k):
+        view = out_ref.at[pl.ds(line_of(k) * 4, 4), 1 - h]
+        return remote(view, view, share_send.at[k], share_recv.at[k], sibling)
+
+    def starts_of(token):
+        first = jnp.zeros_like(token)
+        offset = jnp.full_like(token, req_offset_ref[0])
+        end = req_len_ref[0]
+        for r in range(1, req_len_ref.shape[0]):
+            later = token >= end
+            first = jnp.where(later, end, first)
+            offset = jnp.where(later, req_offset_ref[r], offset)
+            end = end + req_len_ref[r]
+        return first, offset
+
+    def turns(token):
+        first, offset = starts_of(token)
+        angle = (offset + token - first).astype(f32) * freq_ref[...]
+        lane = iota(angle.shape, 1)
+        sine = jnp.sin(angle)
+        sine = jnp.where(lane < ROPE // 2, -sine, sine)
+        rotary = lane < ROPE
+        return jnp.where(rotary, jnp.cos(angle), 0.0), jnp.where(rotary, sine, 0.0)
+
+    def spin(values, turn):
+        lane = iota(values.shape, 1)
+        other = jnp.where(
+            lane < ROPE // 2,
+            pltpu.roll(values, 128 - ROPE // 2, 1),
+            pltpu.roll(values, ROPE // 2, 1),
+        )
+        return (values * turn[0] + other * turn[1]).astype(bf16)
+
+    base = s * tok_rows
+    rows = hidden_ref[pl.ds(pl.multiple_of(h * rows_half, rows_half), rows_half), :].astype(f32)
+    inverse = lax.rsqrt(jnp.mean(rows * rows, axis=1, keepdims=True) + EPSILON)
+    normed = (rows * inverse * gain_ref[...]).astype(bf16)
+    full = lax.dot_general(normed, kv_ref[:KV_RANK], pair, preferred_element_type=f32)
+    end = lax.dot_general(
+        normed, kv_ref[KV_RANK + ROPE - 128 :], pair, preferred_element_type=f32
+    )
+    inverse = lax.rsqrt(jnp.mean(full * full, axis=1, keepdims=True) + EPSILON)
+    out_ref[s, h, :, :KV_RANK] = (full * inverse * kv_gain_ref[...]).astype(bf16)
+    half_token = base + h * rows_half + iota((rows_half, 1), 0)
+    key_rope = spin(pltpu.roll(end, ROPE, 1), turns(half_token))
+    named = jnp.zeros((128, tok_rows), f32)
+    place = iota(named.shape, 0) - ROPE
+    for k in range(ids_ref.shape[0]):
+        named = jnp.where(ids_ref[k : k + 1, :] == place, 1.0, named)
+    row_pick = iota((rows_half, tok_rows), 1) == h * rows_half + iota((rows_half, tok_rows), 0)
+    row_pick = jnp.where(row_pick, 1.0, 0.0).astype(bf16)
+    mask = lax.dot_general(row_pick, named.astype(bf16), pair, preferred_element_type=f32)
+    out_ref[s, h, :, KV_RANK:] = (key_rope.astype(f32) + mask).astype(bf16)
+    pl.semaphore_wait(barrier, len(peers))
+
+    def ring(t):
+        @pl.when((t >= 1) & (t <= z))
+        def _():
+            up_in(t).wait_recv()
+
+        @pl.when((t <= z) & (z < 3))
+        def _():
+            up(t).start()
+
+        @pl.when((t >= 1) & (t <= 3 - z))
+        def _():
+            low_in(t).wait_recv()
+
+        @pl.when((t <= 3 - z) & (z > 0))
+        def _():
+            low(t).start()
+
+        for step in (3, 1, 2):
+            plane(t, step).start()
+
+    def meet_rows(k):
+        for step in (1, 2, 3):
+            plane_in(k, step).wait_recv()
+        share(k).start()
+
+    ring(0)
+    token = base + iota((tok_rows, 1), 0)
+    turn = turns(token)
+    loads[0].wait()
+    loads[1].wait()
+    for two in range(heads // 2):
+        left = queries[:, 384 * two : 384 * two + 128]
+        middle = queries[:, 384 * two + 128 : 384 * two + 256].astype(f32)
+        right = queries[:, 384 * two + 256 : 384 * two + 384].astype(f32)
+        lane = iota(middle.shape, 1)
+        turned = pltpu.roll(right, 64, 1)
+        nope = jnp.where(lane < 64, pltpu.roll(middle, 64, 1), turned).astype(bf16)
+        for odd, columns, rotary in ((0, left, middle), (1, nope, turned)):
+            head = 2 * two + odd
+            here = slice(head * tok_rows, (head + 1) * tok_rows)
+            query[here, :KV_RANK] = jnp.dot(
+                columns, key_up[head], preferred_element_type=f32
+            ).astype(bf16)
+            query[here, KV_RANK:] = spin(rotary, turn)
+    peak[...] = jnp.full_like(peak, MASKED)
+    total[...] = jnp.zeros_like(total)
+    acc[...] = jnp.zeros_like(acc)
+    first = jnp.concatenate([starts_of(token)[0]] * part_heads, axis=0)
+    own = jnp.concatenate([token] * part_heads, axis=0)
+    scale = math.log2(math.e) / math.sqrt(NOPE + ROPE)
+
+    def attend(k, part_no):
+        line = line_of(k)
+        keys = out_ref[pl.ds(line * 4, 4)].reshape(tile_keys, out_ref.shape[3])
+        here = slice(part_no * part_rows, (part_no + 1) * part_rows)
+        scores = scale * lax.dot_general(query[here, :], keys, pair, preferred_element_type=f32)
+        index = line * tile_keys + iota(scores.shape, 1)
+        scores = jnp.where((index <= own) & (index >= first), scores, MASKED)
+        old = peak[part_no, :, :1]
+        new = jnp.maximum(old, jnp.max(scores, axis=1, keepdims=True))
+        terms = jnp.exp2(scores - new)
+        fade = jnp.exp2(old - new)
+        total[part_no, :, :1] = total[part_no, :, :1] * fade + jnp.sum(
+            terms, axis=1, keepdims=True
+        )
+        peak[part_no, :, :1] = new
+        acc[part_no] = acc[part_no] * fade + jnp.dot(
+            terms.astype(bf16), keys[:, :KV_RANK], preferred_element_type=f32
+        )
+
+    ring(1)
+    meet_rows(0)
+
+    @pl.loop(0, 4)
+    def _(k):
+        share_in(k).wait_recv()
+
+        @pl.when(k <= z)
+        def _():
+            attend(k, 0)
+
+        @pl.when(k <= 1)
+        def _():
+            ring(k + 2)
+
+        @pl.when(k <= 2)
+        def _():
+            meet_rows(k + 1)
+
+        @pl.when(k <= z)
+        def _():
+            attend(k, 1)
+
+    loads[2].wait()
+    loads[3].wait()
     for head in range(heads):
-        here = slice(head * tok_rows, (head + 1) * tok_rows)
-        query[here, :KV_RANK] = jnp.dot(
-            nope_ref[head], key_up_ref[head], preferred_element_type=jnp.float32
-        ).astype(jnp.bfloat16)
-        query[here, KV_RANK:] = rope_ref[head]
-    first = jnp.concatenate([first_ref[...]] * group, axis=0)
-    own = span_ref[2] + lax.broadcasted_iota(jnp.int32, (tok_rows, 1), 0)
-    own = jnp.concatenate([own] * group, axis=0)
-
-    @pl.loop(0, heads // group)
-    def _(part_no):
-        base = pl.multiple_of(part_no * group_rows, group_rows)
-        here = pl.ds(base, group_rows)
-        peak[...] = jnp.full_like(peak, MASKED)
-        total[...] = jnp.zeros_like(total)
-        acc[...] = jnp.zeros_like(acc)
-
-        @pl.loop(span_ref[0], span_ref[1])
-        def _(tile):
-            start = pl.multiple_of(tile * key_tile, key_tile)
-            keys = keys_ref[pl.ds(start, key_tile), :]
-            scores = score_scale * lax.dot_general(
-                query[here, :], keys, contract, preferred_element_type=jnp.float32
-            )
-            index = start + lax.broadcasted_iota(jnp.int32, scores.shape, 1)
-            allowed = (index <= own) & (index >= first)
-            scores = jnp.where(allowed, scores, MASKED)
-            old = peak[:, :1]
-            new = jnp.maximum(old, jnp.max(scores, axis=1, keepdims=True))
-            terms = jnp.where(allowed, jnp.exp(scores - new), 0.0)
-            fade = jnp.exp(old - new)
-            total[:, :1] = total[:, :1] * fade + jnp.sum(terms, axis=1, keepdims=True)
-            peak[:, :1] = new
-            acc[...] = acc[...] * fade + jnp.dot(
-                terms.astype(jnp.bfloat16), keys[:, :KV_RANK], preferred_element_type=jnp.float32
-            )
-
-        attended = (acc[...] / total[:, :1]).astype(jnp.bfloat16)
-        for member in range(group):
-            heads_buf[part_no * group + member] = jnp.dot(
-                attended[member * tok_rows : (member + 1) * tok_rows],
-                value_up_ref[part_no * group + member],
-                preferred_element_type=jnp.float32,
-            ).astype(jnp.bfloat16)
-
-    joined = jnp.concatenate([heads_buf[head] for head in range(heads)], axis=1)
-    out_ref[...] = jnp.dot(
-        joined, out_proj_ref[...], preferred_element_type=jnp.float32
-    ).astype(out_ref.dtype)
-
-
-def attend_rows(nope, rope, keys, key_up, value_up, out_proj, first, first_token):
-    heads, tok_rows = nope.shape[0], nope.shape[1]
-    key_tile = 512 if keys.shape[0] % 512 == 0 else 128
-    width = keys.shape[1]
-    span = jnp.stack(
-        [
-            jnp.min(first) // key_tile,
-            (first_token + tok_rows + key_tile - 1) // key_tile,
-            first_token,
+        part_no, member = head // part_heads, head % part_heads
+        here = slice(member * tok_rows, (member + 1) * tok_rows)
+        attended = (acc[part_no, here, :] / total[part_no, here, :1]).astype(bf16)
+        heads_buf[:, head * V_HEAD : (head + 1) * V_HEAD] = jnp.dot(
+            attended, value_up[head], preferred_element_type=f32
+        ).astype(bf16)
+    attn_ref[...] = jnp.dot(
+        heads_buf[...], out_proj[...], preferred_element_type=f32
+    ).astype(attn_ref.dtype)
+
+    @pl.loop(0, 4)
+    def _(k):
+        @pl.when((k <= z) & (z < 3))
+        def _():
+            up(k).wait_send()
+
+        @pl.when((k <= 3 - z) & (z > 0))
+        def _():
+            low(k).wait_send()
+
+        for step in (1, 2, 3):
+            plane(k, step).wait_send()
+        share(k).wait_send()
+
+
+def front(
+    req_len,
+    req_offset,
+    hidden,
+    attn_gain,
+    kv_down,
+    kv_gain,
+    expert_ids,
+    queries,
+    key_up,
+    value_up,
+    out_proj,
+    seq_count,
+):
+    tok_rows = hidden.shape[0]
+    heads = key_up.shape[0]
+    width = KV_RANK + 128
+    lanes = np.arange(128) % (ROPE // 2)
+    frequency = np.exp(-math.log(ROPE_BASE) * lanes * (2.0 / ROPE)).astype(np.float32)[None, :]
+    bf16, f32 = jnp.bfloat16, jnp.float32
+    vmem = pl.BlockSpec(memory_space=pltpu.VMEM)
+    smem = pl.BlockSpec(memory_space=pltpu.SMEM)
+    hbm = pl.BlockSpec(memory_space=pl.ANY)
+    dma = pltpu.SemaphoreType.DMA
+    part_rows = heads * tok_rows // 2
+    return pl.pallas_call(
+        front_kernel,
+        out_shape=(
+            jax.ShapeDtypeStruct((seq_count, 2, tok_rows // 2, width), bf16),
+            jax.ShapeDtypeStruct((tok_rows, out_proj.shape[1]), bf16),
+        ),
+        in_specs=[smem] * 2 + [vmem] * 6 + [hbm] * 4,
+        out_specs=(vmem, vmem),
+        scratch_shapes=[
+            pltpu.VMEM(queries.shape, bf16),
+            pltpu.VMEM(key_up.shape, bf16),
+            pltpu.VMEM(value_up.shape, bf16),
+            pltpu.VMEM(out_proj.shape, bf16),
+            pltpu.VMEM((heads * tok_rows, width), bf16),
+            pltpu.VMEM((2, part_rows, KV_RANK), f32),
+            pltpu.VMEM((2, part_rows, 128), f32),
+            pltpu.VMEM((2, part_rows, 128), f32),
+            pltpu.VMEM((tok_rows, heads * V_HEAD), bf16),
         ]
-    ).astype(jnp.int32)
-    vmem = pl.BlockSpec(memory_space=pltpu.VMEM)
-    rows = 4 * tok_rows
-    return pl.pallas_call(
-        functools.partial(attend_kernel, key_tile),
-        out_shape=jax.ShapeDtypeStruct((tok_rows, out_proj.shape[1]), jnp.bfloat16),
-        in_specs=[pl.BlockSpec(memory_space=pltpu.SMEM)] + [vmem] * 7,
-        out_specs=vmem,
-        scratch_shapes=[
-            pltpu.VMEM((heads * tok_rows, width), jnp.bfloat16),
-            pltpu.VMEM((rows, KV_RANK), jnp.float32),
-            pltpu.VMEM((rows, 128), jnp.float32),
-            pltpu.VMEM((rows, 128), jnp.float32),
-            pltpu.VMEM((heads, tok_rows, V_HEAD), jnp.bfloat16),
-        ],
-        compiler_params=pltpu.CompilerParams(vmem_limit_bytes=40 * 1024 * 1024),
-    )(span, first[:, None], nope, rope, keys, key_up, value_up, out_proj)
+        + [dma((size,)) for size in [4] + [4] * 4 + [12] * 2 + [4] * 2],
+        compiler_params=pltpu.CompilerParams(
+            collective_id=0, has_side_effects=True, vmem_limit_bytes=60 * 1024 * 1024
+        ),
+    )(
+        req_len,
+        req_offset,
+        jnp.asarray(frequency),
+        hidden,
+        attn_gain[None, :],
+        kv_down.T,
+        kv_gain[None, :],
+        expert_ids.T,
+        queries,
+        key_up,
+        value_up,
+        out_proj,
+    )
 
 
 def body(
@@ -766,26 +883,21 @@
     seq_count = lax.axis_size("seq")
     fast = seq_count == 16 and head_count == 2 and expert_count == 16
     if fast:
-        route_mask = jnp.any(expert_ids[:, :, None] == expert_axis[None, None, :], axis=1)
-        payload = jnp.concatenate([latent, key_rope, route_mask.astype(jnp.bfloat16)], axis=1)
-        payload = jnp.pad(payload, ((0, 0), (0, -payload.shape[1] % 128)))
-        gathered = gather_rows(payload, seq_count)
-        by_head = jnp.swapaxes(head_view, 0, 1)
-        rope_pad = gathered.shape[1] - KV_RANK - ROPE
-        by_head_rope = jnp.pad(jnp.swapaxes(query_rope, 0, 1), ((0, 0), (0, 0), (0, rope_pad)))
-        req_ends = running(req_len)
-        member = my_request[:, None] == jnp.arange(req_len.shape[0])[None, :]
-        first = jnp.sum(jnp.where(member, (req_ends - req_len)[None, :], 0), axis=1)
-        attn_part = attend_rows(
-            by_head[:, :, :NOPE],
-            by_head_rope,
-            gathered,
+        blocks, attn_part = front(
+            req_len,
+            req_offset,
+            hidden,
+            attn_gain,
+            kv_down,
+            kv_gain,
+            expert_ids,
+            queries,
             key_up,
             value_up,
             out_proj,
-            first,
-            seq_place * tok_rows,
-        )
+            seq_count,
+        )
+        gathered = blocks.reshape(seq_count * tok_rows, blocks.shape[3])
         source_row = source_block[:, None] * BLOCK + jnp.arange(BLOCK, dtype=jnp.int32)[None, :]
         pick_rows = source_row[:, :, None] == jnp.arange(gathered.shape[0], dtype=jnp.int32)
         pick_rows = (pick_rows & slot_filled[:, None, None]).reshape(DEC_SLOTS * BLOCK, -1)

time: 141 us -> 119 us (0.84)
  other arithmetic: 9.6 us -> 1.76 us
  local copies, waits for them, and re-layouts: 11.9 us -> 5.11 us
  Pallas kernels: 113 us -> 108 us
  between operations: 3.46 us -> 0.67 us
    reduce_sum x5 -> x0, other arithmetic: 3.09 us -> none  [the longest x2 1.31 us: rms_rows(): jnp.mean(values * values, axis=-1, keepdims=True) + EPSILON]
    pallas_call x1, Pallas kernels: 80.9 us -> 78.5 us  [expert_layer(): pl.pallas_call(expert_kernel, out_shape=jax.ShapeDtypeStruct((tok_rows, h...]
    pallas_call x2 -> x1, Pallas kernels: 32.3 us -> 29.9 us  [front(): pl.pallas_call(front_kernel, out_shape=(jax.ShapeDtypeStruct((seq_count,...]
    convert_element_type x1 -> x0, local copies, waits for them, and re-layouts: 1.92 us -> none  [rotate(): first_half = values[..., :half_width].astype(jnp.float32)]
    dot_general x1 -> x0, matrix products: 1.89 us -> none  [body(): kv_full = jnp.dot(normed, kv_down, preferred_element_type=jnp.float32)]
    another operation x3 -> x0, other arithmetic: 1.76 us -> none
    slice x1 -> x0, local copies, waits for them, and re-layouts: 1.76 us -> none  [body(): by_head[:, :, :NOPE]]
    dot_general x1, matrix products: 0.62 us -> 2.36 us  [body(): jnp.dot(pick_rows.astype(jnp.bfloat16), gathered, preferred_element_type=...]
where the time goes in v2:
time: 119 us; the launch traced here: 118 us
  Pallas kernels  108 us (91%)
  local copies, waits for them, and re-layouts  5.11 us (4%)
  matrix products  2.36 us (2%)
  other arithmetic  1.76 us (1%)
    pallas_call x1, Pallas kernels, expert_layer(): pl.pallas_call(expert_kernel, out_shape=jax.ShapeDtypeStruct((tok_rows, h...  78.5 us
    pallas_call x1, Pallas kernels, front(): pl.pallas_call(front_kernel, out_shape=(jax.ShapeDtypeStruct((seq_count,...  29.9 us

profile of v2, /device:TPU:0, one launch (start us, length us, event | category | flops | bytes accessed | tf_op | source)
XLA Modules:
  0.0 118.3 jit_solution(13494351400446340053)
XLA Ops:
  0.6 0.8 fusion.4
  1.5 0.1 iota_add_fusion
  1.6 0.1 add.39
  1.7 0.8 compare_reduce_fusion
  2.5 0.1 and.15
  2.6 0.1 and.16
  2.7 29.9 %shard_map.184 = (bf16[16,2,64,640]{3,2,1,0:T(8,128)(2,1)}, bf16[128,2048]{1,0:T(8,128)(2,1)}) custom-call(s32[2]{0:T(128)} %req_len_ref.1, s32[2]{0:T(128)} %req_offset_ref.1, f32[1,128]{1,0:T(1,128)} %constant.20.clone.freq_ref, bf16[128,2048]{1,0:T(8,128)(2,1)} %hidden_ref.3, f32[1,2048]{1,0:T(1,128)} %bitcast.22, bf16[576,2048]{1,0:T(8,128)(2,1)} %bitcast.18, ...), custom_call_target="tpu_custom_call" | custom-call | tf_op jit(solution)/shard_map/pallas_call | solution.py:792
  32.6 2.4 %convolution_convert_fusion = bf16[64,640]{1,0:T(8,128)(2,1)S(1)} fusion(bf16[2048,640]{1,0:T(8,128)(2,1)} %bitcast.15, s32[64]{0:T(128)S(1)} %add.39, pred[64]{0:T(512)(128)(4,1)S(1)} %and.16), kind=kOutput, calls=%fused_computation | convolution fusion | flops 168075264 | bytes 2703680 | tf_op jit(solution)/shard_map/dot_general | solution.py:904
  35.0 0.6 slice.13
  35.6 0.7 reshape.53
  36.3 1.9 %slice.12 = bf16[2048,128]{1,0:T(8,128)(2,1)} slice(bf16[2048,640]{1,0:T(8,128)(2,1)} %bitcast.16), slice={[0:2048], [512:640]} | slice | bytes 1048576 | tf_op jit(solution)/shard_map/slice | solution.py:909
  38.1 78.5 %shard_map.185 = bf16[128,1024]{1,0:T(8,128)(2,1)} custom-call(bf16[128,2048]{1,0:T(8,128)(2,1)} %hidden_ref.3, bf16[128,2048]{1,0:T(8,128)(2,1)} %get-tuple-element.5.attn_ref, f32[1,2048]{1,0:T(1,128)} %bitcast.23, bf16[16,128,128]{2,1,0:T(8,128)(2,1)} %bitcast.19, f32[16,2048]{1,0:T(8,128)} %bitcast.20, bf16[2,704,2048]{2,1,0:T(8,128)(2,1)} %bitcast.14, ...), custom_call_target="tpu_custom_call" | custom-call | tf_op jit(solution)/shard_map/pallas_call | solution.py:455
  116.6 1.7 %copy.21 = bf16[128,1024]{1,0:T(8,128)(2,1)} copy(bf16[128,1024]{1,0:T(8,128)(2,1)} %shard_map.185) | data formatting | bytes 524288
  (3 shorter events, 0.0 us)

commit v3 on v1

--- a/solution.py
+++ b/solution.py
@@ -3,6 +3,7 @@
 
 import jax
 import jax.numpy as jnp
+import numpy as np
 from jax import lax
 from jax.experimental import pallas as pl
 from jax.experimental.pallas import tpu as pltpu
@@ -92,133 +93,6 @@
     return place + step * (1 - 2 * lax.rem(lax.div(place, step), 2))
 
 
-def place_of(s, h, nz, back, turn):
-    line = lax.rem(lax.div(s, 4) - back + nz, nz)
-    block = line * 4 + lax.rem(s, 4)
-    if turn & 1:
-        block = flip(block, 2 - h)
-    if turn & 2:
-        block = flip(block, 1 + h)
-    return block
-
-
-def meet(s, h, nz):
-    barrier = pltpu.get_barrier_semaphore()
-    peers = [(place_of(s, h, nz, back, 0), h) for back in range(1, nz)]
-    peers += [(flip(s, 2 - h), h), (flip(s, 1 + h), h), (s, 1 - h)]
-    for peer in peers:
-        pl.semaphore_signal(barrier, inc=1, device_id=peer, device_id_type=MESH)
-    pl.semaphore_wait(barrier, len(peers))
-
-
-class Spread:
-    def __init__(self, buf, s, h, nz, sems, blocks_first=False):
-        self.blocks_first = blocks_first
-        self.buf, self.s, self.h, self.nz = buf, s, h, nz
-        self.sems = sems
-
-    def move(self, block, kind, index, device):
-        view = self.buf.at[block, self.h] if self.blocks_first else self.buf.at[self.h, block]
-        return pltpu.make_async_remote_copy(
-            src_ref=view,
-            dst_ref=view,
-            send_sem=self.sems[2 * kind].at[index],
-            recv_sem=self.sems[2 * kind + 1].at[index],
-            device_id=device,
-            device_id_type=MESH,
-        )
-
-    def block(self, back, turn):
-        return place_of(self.s, self.h, self.nz, back, turn)
-
-    def line(self, ahead):
-        device = (place_of(self.s, self.h, self.nz, self.nz - ahead, 0), self.h)
-        return self.move(self.block(0, 0), 0, ahead, device)
-
-    def line_in(self, back):
-        return self.move(self.block(back, 0), 0, back, (self.s, 1 - self.h))
-
-    def second(self, back, turn=0):
-        return self.move(self.block(back, turn), 1, back, (flip(self.s, 2 - self.h), self.h))
-
-    def third(self, back, side, turn=0):
-        device = (flip(self.s, 1 + self.h), self.h)
-        return self.move(self.block(back, turn + side), 2, 2 * back + side, device)
-
-    def sibling(self, back, mine):
-        half = self.h if mine else 1 - self.h
-        line = lax.rem(lax.div(self.s, 4) - back + self.nz, self.nz)
-        four = pl.ds(line * 4, 4)
-        view = self.buf.at[four, half] if self.blocks_first else self.buf.at[half, four]
-        return pltpu.make_async_remote_copy(
-            src_ref=view,
-            dst_ref=view,
-            send_sem=self.sems[6].at[back],
-            recv_sem=self.sems[7].at[back],
-            device_id=(self.s, 1 - self.h),
-            device_id_type=MESH,
-        )
-
-    def send_all(self):
-        for ahead in range(1, self.nz):
-            self.line(ahead).start()
-        for back in range(self.nz):
-            if back:
-                self.line_in(back).wait_recv()
-            self.third(back, 0).start()
-            self.second(back).start()
-            self.second(back, 1).wait_recv()
-            self.third(back, 1).start()
-
-    def pass_on(self, back):
-        for side in range(2):
-            self.third(back, side, 2).wait_recv()
-        self.sibling(back, True).start()
-
-    def drain(self):
-        for ahead in range(1, self.nz):
-            self.line(ahead).wait_send()
-        for back in range(self.nz):
-            self.second(back).wait_send()
-            self.third(back, 0).wait_send()
-            self.third(back, 1).wait_send()
-            self.sibling(back, True).wait_send()
-
-
-def spread_sems(nz):
-    dma = pltpu.SemaphoreType.DMA
-    return [dma((nz,)), dma((nz,)), dma((nz,)), dma((nz,)), dma((2 * nz,)), dma((2 * nz,)), dma((nz,)), dma((nz,))]
-
-
-def gather_kernel(nz, rows_ref, out_ref, *sems):
-    s, h = lax.axis_index("seq"), lax.axis_index("head")
-    out_ref[s, h] = rows_ref[h]
-    meet(s, h, nz)
-    spread = Spread(out_ref, s, h, nz, sems, True)
-    spread.send_all()
-    for back in range(nz):
-        spread.pass_on(back)
-    for back in range(nz):
-        spread.sibling(back, False).wait_recv()
-    spread.drain()
-
-
-def gather_rows(rows, seq_count):
-    tok_rows, width = rows.shape
-    nz = seq_count // 4
-    out = pl.pallas_call(
-        functools.partial(gather_kernel, nz),
-        out_shape=jax.ShapeDtypeStruct((seq_count, 2, tok_rows // 2, width), rows.dtype),
-        in_specs=[pl.BlockSpec(memory_space=pltpu.VMEM)],
-        out_specs=pl.BlockSpec(memory_space=pltpu.VMEM),
-        scratch_shapes=spread_sems(nz),
-        compiler_params=pltpu.CompilerParams(
-            collective_id=0, has_side_effects=True, vmem_limit_bytes=16 * 1024 * 1024
-        ),
-    )(rows.reshape(2, tok_rows // 2, width))
-    return out.reshape(seq_count * tok_rows, width)
-
-
 def line_place(line, s):
     return line * 4 + lax.rem(s, 4)
 
@@ -239,15 +113,37 @@
     return line + upper * (3 - 2 * line)
 
 
-def expert_kernel(
+def layer_kernel(
+    req_len_ref,
+    req_offset_ref,
+    freq_ref,
     hidden_ref,
-    attn_ref,
     gain_ref,
-    tail_ref,
+    kv_ref,
+    kv_gain_ref,
+    ids_ref,
+    slot_ref,
+    ffn_gain_ref,
     router_ref,
+    queries_hbm,
+    key_up_hbm,
+    value_up_hbm,
+    out_proj_hbm,
     gate_up_hbm,
     down_hbm,
     out_ref,
+    decode_ref,
+    keys_buf,
+    queries,
+    key_up,
+    value_up,
+    out_proj,
+    query,
+    acc,
+    peak,
+    total,
+    heads_buf,
+    attn_buf,
     attn_in,
     mixed,
     x_buf,
@@ -265,7 +161,16 @@
     gate_up,
     down,
     load_sem,
-    attn_sem,
+    ku_send,
+    ku_recv,
+    kl_send,
+    kl_recv,
+    plane_send,
+    plane_recv,
+    share_keys_send,
+    share_keys_recv,
+    swap_send,
+    swap_recv,
     up_send,
     up_recv,
     down_send,
@@ -283,18 +188,30 @@
 ):
     s, h = lax.axis_index("seq"), lax.axis_index("head")
     z, c = lax.div(s, 4), lax.rem(s, 4)
-    cols = hidden_ref.shape[1]
-    half = cols // 2
-    slots = stage.shape[2]
+    bf16, f32 = jnp.bfloat16, jnp.float32
+    pair = (((1,), (1,)), ((), ()))
     tok_rows = hidden_ref.shape[0]
-    expert_count = router_ref.shape[0]
+    rows_half = tok_rows // 2
+    heads = key_up.shape[0]
+    part_heads = heads // 2
+    part_rows = part_heads * tok_rows
+    tile_keys = 4 * tok_rows
     sibling = (s, 1 - h)
-    loads = [
-        pltpu.make_async_copy(gate_up_hbm, gate_up, load_sem.at[0]),
-        pltpu.make_async_copy(down_hbm, down, load_sem.at[1]),
-    ]
+    pairs = [(queries_hbm, queries), (key_up_hbm, key_up)]
+    pairs += [(value_up_hbm, value_up), (out_proj_hbm, out_proj)]
+    pairs += [(gate_up_hbm, gate_up), (down_hbm, down)]
+    loads = [pltpu.make_async_copy(*both, load_sem.at[i]) for i, both in enumerate(pairs)]
     for load in loads:
         load.start()
+
+    barrier = pltpu.get_barrier_semaphore()
+    peers = [(line_place(lax.rem(z + back, 4), s), h) for back in range(1, 4)]
+    peers += [(across(s, step), h) for step in range(1, 4)] + [sibling]
+    for peer in peers:
+        pl.semaphore_signal(barrier, inc=1, device_id=peer, device_id_type=MESH)
+
+    def iota(shape, dim):
+        return lax.broadcasted_iota(jnp.int32, shape, dim)
 
     def remote(src, dst, send, recv, device):
         return pltpu.make_async_remote_copy(
@@ -306,13 +223,217 @@
             device_id_type=MESH,
         )
 
-    barrier = pltpu.get_barrier_semaphore()
-    peers = [(line_place(lax.rem(z + back, 4), s), h) for back in range(1, 4)]
-    peers += [(across(s, step), h) for step in range(1, 4)] + [sibling]
-    for peer in peers:
-        pl.semaphore_signal(barrier, inc=1, device_id=peer, device_id_type=MESH)
+    def key_up_move(t):
+        view = keys_buf.at[(z - t) * 4 + c, h]
+        device = (line_place(lax.rem(z + 1, 4), s), h)
+        return remote(view, view, ku_send.at[t], ku_recv.at[t], device)
+
+    def key_up_in(t):
+        view = keys_buf.at[(z - t) * 4 + c, h]
+        return remote(view, view, ku_send.at[t - 1], ku_recv.at[t - 1], sibling)
+
+    def key_low_move(t):
+        view = keys_buf.at[(z + t) * 4 + c, h]
+        device = (line_place(lax.rem(z + 3, 4), s), h)
+        return remote(view, view, kl_send.at[t], kl_recv.at[t], device)
+
+    def key_low_in(t):
+        view = keys_buf.at[(z + t) * 4 + c, h]
+        return remote(view, view, kl_send.at[t - 1], kl_recv.at[t - 1], sibling)
+
+    def line_of(k):
+        return jnp.where(k <= z, z - k, k)
+
+    def plane(k, step):
+        view = keys_buf.at[line_of(k) * 4 + c, h]
+        index = 3 * k + step - 1
+        device = (across(s, step), h)
+        return remote(view, view, plane_send.at[index], plane_recv.at[index], device)
+
+    def plane_in(k, step):
+        view = keys_buf.at[line_of(k) * 4 + lax.rem(across(s, step), 4), h]
+        index = 3 * k + step - 1
+        return remote(view, view, plane_send.at[index], plane_recv.at[index], sibling)
+
+    def share_keys(k):
+        view = keys_buf.at[pl.ds(line_of(k) * 4, 4), h]
+        return remote(view, view, share_keys_send.at[k], share_keys_recv.at[k], sibling)
+
+    def share_keys_in(k):
+        view = keys_buf.at[pl.ds(line_of(k) * 4, 4), 1 - h]
+        return remote(view, view, share_keys_send.at[k], share_keys_recv.at[k], sibling)
+
+    def starts_of(token):
+        first = jnp.zeros_like(token)
+        offset = jnp.full_like(token, req_offset_ref[0])
+        end = req_len_ref[0]
+        for r in range(1, req_len_ref.shape[0]):
+            later = token >= end
+            first = jnp.where(later, end, first)
+            offset = jnp.where(later, req_offset_ref[r], offset)
+            end = end + req_len_ref[r]
+        return first, offset
+
+    def turns(token):
+        first, offset = starts_of(token)
+        angle = (offset + token - first).astype(f32) * freq_ref[...]
+        lane = iota(angle.shape, 1)
+        sine = jnp.sin(angle)
+        sine = jnp.where(lane < ROPE // 2, -sine, sine)
+        rotary = lane < ROPE
+        return jnp.where(rotary, jnp.cos(angle), 0.0), jnp.where(rotary, sine, 0.0)
+
+    def spin(values, turn):
+        lane = iota(values.shape, 1)
+        other = jnp.where(
+            lane < ROPE // 2,
+            pltpu.roll(values, 128 - ROPE // 2, 1),
+            pltpu.roll(values, ROPE // 2, 1),
+        )
+        return (values * turn[0] + other * turn[1]).astype(bf16)
+
+    base = s * tok_rows
+    rows = hidden_ref[pl.ds(pl.multiple_of(h * rows_half, rows_half), rows_half), :].astype(f32)
+    inverse = lax.rsqrt(jnp.mean(rows * rows, axis=1, keepdims=True) + EPSILON)
+    normed = (rows * inverse * gain_ref[...]).astype(bf16)
+    full = lax.dot_general(normed, kv_ref[:KV_RANK], pair, preferred_element_type=f32)
+    end = lax.dot_general(
+        normed, kv_ref[KV_RANK + ROPE - 128 :], pair, preferred_element_type=f32
+    )
+    inverse = lax.rsqrt(jnp.mean(full * full, axis=1, keepdims=True) + EPSILON)
+    keys_buf[s, h, :, :KV_RANK] = (full * inverse * kv_gain_ref[...]).astype(bf16)
+    half_token = base + h * rows_half + iota((rows_half, 1), 0)
+    key_rope = spin(pltpu.roll(end, ROPE, 1), turns(half_token))
+    named = jnp.zeros((128, tok_rows), f32)
+    place = iota(named.shape, 0) - ROPE
+    for k in range(ids_ref.shape[0]):
+        named = jnp.where(ids_ref[k : k + 1, :] == place, 1.0, named)
+    row_pick = iota((rows_half, tok_rows), 1) == h * rows_half + iota((rows_half, tok_rows), 0)
+    row_pick = jnp.where(row_pick, 1.0, 0.0).astype(bf16)
+    mask = lax.dot_general(row_pick, named.astype(bf16), pair, preferred_element_type=f32)
+    keys_buf[s, h, :, KV_RANK:] = (key_rope.astype(f32) + mask).astype(bf16)
     pl.semaphore_wait(barrier, len(peers))
 
+    def key_ring(t):
+        @pl.when((t >= 1) & (t <= z))
+        def _():
+            key_up_in(t).wait_recv()
+
+        @pl.when((t <= z) & (z < 3))
+        def _():
+            key_up_move(t).start()
+
+        @pl.when((t >= 1) & (t <= 3 - z))
+        def _():
+            key_low_in(t).wait_recv()
+
+        @pl.when((t <= 3 - z) & (z > 0))
+        def _():
+            key_low_move(t).start()
+
+        for step in (3, 1, 2):
+            plane(t, step).start()
+
+    def meet_keys(k):
+        for step in (1, 2, 3):
+            plane_in(k, step).wait_recv()
+        share_keys(k).start()
+
+    key_ring(0)
+    token = base + iota((tok_rows, 1), 0)
+    turn = turns(token)
+    loads[0].wait()
+    loads[1].wait()
+    for two in range(heads // 2):
+        left = queries[:, 384 * two : 384 * two + 128]
+        middle = queries[:, 384 * two + 128 : 384 * two + 256].astype(f32)
+        right = queries[:, 384 * two + 256 : 384 * two + 384].astype(f32)
+        lane = iota(middle.shape, 1)
+        turned = pltpu.roll(right, 64, 1)
+        nope = jnp.where(lane < 64, pltpu.roll(middle, 64, 1), turned).astype(bf16)
+        for odd, columns, rotary in ((0, left, middle), (1, nope, turned)):
+            head = 2 * two + odd
+            here = slice(head * tok_rows, (head + 1) * tok_rows)
+            query[here, :KV_RANK] = jnp.dot(
+                columns, key_up[head], preferred_element_type=f32
+            ).astype(bf16)
+            query[here, KV_RANK:] = spin(rotary, turn)
+    peak[...] = jnp.full_like(peak, MASKED)
+    total[...] = jnp.zeros_like(total)
+    acc[...] = jnp.zeros_like(acc)
+    first = jnp.concatenate([starts_of(token)[0]] * part_heads, axis=0)
+    own = jnp.concatenate([token] * part_heads, axis=0)
+    scale = math.log2(math.e) / math.sqrt(NOPE + ROPE)
+
+    def attend(k, part_no):
+        line = line_of(k)
+        keys = keys_buf[pl.ds(line * 4, 4)].reshape(tile_keys, keys_buf.shape[3])
+        here = slice(part_no * part_rows, (part_no + 1) * part_rows)
+        scores = scale * lax.dot_general(query[here, :], keys, pair, preferred_element_type=f32)
+        index = line * tile_keys + iota(scores.shape, 1)
+        scores = jnp.where((index <= own) & (index >= first), scores, MASKED)
+        old = peak[part_no, :, :1]
+        new = jnp.maximum(old, jnp.max(scores, axis=1, keepdims=True))
+        terms = jnp.exp2(scores - new)
+        fade = jnp.exp2(old - new)
+        total[part_no, :, :1] = total[part_no, :, :1] * fade + jnp.sum(
+            terms, axis=1, keepdims=True
+        )
+        peak[part_no, :, :1] = new
+        acc[part_no] = acc[part_no] * fade + jnp.dot(
+            terms.astype(bf16), keys[:, :KV_RANK], preferred_element_type=f32
+        )
+
+    key_ring(1)
+    meet_keys(0)
+
+    @pl.loop(0, 4)
+    def _(k):
+        share_keys_in(k).wait_recv()
+
+        @pl.when(k <= z)
+        def _():
+            attend(k, 0)
+
+        @pl.when(k <= 1)
+        def _():
+            key_ring(k + 2)
+
+        @pl.when(k <= 2)
+        def _():
+            meet_keys(k + 1)
+
+        @pl.when(k <= z)
+        def _():
+            attend(k, 1)
+
+    loads[2].wait()
+    loads[3].wait()
+    for head in range(heads):
+        part_no, member = head // part_heads, head % part_heads
+        here = slice(member * tok_rows, (member + 1) * tok_rows)
+        attended = (acc[part_no, here, :] / total[part_no, here, :1]).astype(bf16)
+        heads_buf[:, head * V_HEAD : (head + 1) * V_HEAD] = jnp.dot(
+            attended, value_up[head], preferred_element_type=f32
+        ).astype(bf16)
+    cols = hidden_ref.shape[1]
+    half = cols // 2
+
+    def swap(piece):
+        return remote(
+            attn_buf.at[piece],
+            attn_in.at[piece],
+            swap_send.at[piece],
+            swap_recv.at[piece],
+            sibling,
+        )
+
+    for piece in range(2):
+        here = slice(piece * half, (piece + 1) * half)
+        attn_buf[piece] = jnp.dot(
+            heads_buf[...], out_proj[:, here], preferred_element_type=f32
+        ).astype(bf16)
+        swap(piece).start()
     def up(t):
         view = x_buf.at[z - t]
         device = (line_place(lax.rem(z + 1, 4), s), h)
@@ -347,13 +468,15 @@
         view = rows_in.at[k, h, lax.rem(across(s, step), 4)]
         return remote(view, view, go_send.at[index], go_recv.at[index], sibling)
 
-    def share(k):
-        view = rows_in.at[k, h]
-        return remote(view, view, share_send.at[k], share_recv.at[k], sibling)
-
-    def share_in(k):
-        view = rows_in.at[k, 1 - h]
-        return remote(view, view, share_send.at[k], share_recv.at[k], sibling)
+    def share(k, step):
+        view = rows_in.at[k, h, lax.rem(across(s, step), 4)]
+        index = 4 * k + step
+        return remote(view, view, share_send.at[index], share_recv.at[index], sibling)
+
+    def share_in(k, step):
+        view = rows_in.at[k, 1 - h, lax.rem(across(s, step), 4)]
+        index = 4 * k + step
+        return remote(view, view, share_send.at[index], share_recv.at[index], sibling)
 
     def part(k):
         return remote(res.at[k, 1 - h], sib_in.at[k], part_send.at[k], part_recv.at[k], sibling)
@@ -382,25 +505,21 @@
         line = lax.rem(z + back, 4)
         return remote(z_in.at[line], z_in.at[line], home_send.at[0], home_recv.at[line], sibling)
 
-    swap = remote(attn_ref, attn_in, attn_sem.at[0], attn_sem.at[1], sibling)
-    swap.start()
-
-    def iota(shape, dim):
-        return lax.broadcasted_iota(jnp.int32, shape, dim)
-
-    bf16, f32 = jnp.bfloat16, jnp.float32
-    pair = (((1,), (1,)), ((), ()))
+    slots = stage.shape[2]
+    expert_count = router_ref.shape[0]
     four = 4 * slots
-    lane = (tok_rows, 128)
     before = (iota((tok_rows, tok_rows), 0) < iota((tok_rows, tok_rows), 1)).astype(bf16)
     after = (iota((tok_rows, tok_rows), 0) > iota((tok_rows, tok_rows), 1)).astype(bf16)
 
     def one_hot(flags):
         return jnp.where(flags, 1.0, 0.0).astype(bf16)
 
+    def tail_of(block):
+        return keys_buf[block, :, :, KV_RANK:].reshape(tok_rows, 128)
+
     def prepare(k):
         line = turn_line(z, k)
-        tail = tail_ref[line * 4 + c]
+        tail = tail_of(line * 4 + c)
         shape = (four, 128)
         named = one_hot(iota(shape, 1) == ROPE + 4 * z + lax.div(iota(shape, 0), slots))
         slot = lax.rem(iota((four, tok_rows), 0), slots).astype(f32)
@@ -416,7 +535,7 @@
         named = one_hot(iota((slots, 128), 1) == ROPE + s)
         slot = iota((slots, tok_rows), 0).astype(f32)
         for block in range(4):
-            tail = tail_ref[line * 4 + block]
+            tail = tail_of(line * 4 + block)
             member = lax.dot_general(named, tail, pair, preferred_element_type=f32)
             rank = jnp.dot(member.astype(bf16), before, preferred_element_type=f32)
             mine = one_hot((rank == slot) & (member > 0.0))
@@ -435,12 +554,20 @@
     low_pad = jnp.zeros((128 - ROPE - 3 * expert_count, cols), bf16)
     router_buf[...] = jnp.concatenate([top_pad, high, middle, last, low_pad], axis=0)
 
-    swap.wait_recv()
-    total = hidden_ref[...].astype(f32) + (attn_ref[...].astype(f32) + attn_in[...].astype(f32))
-    inverse = lax.rsqrt(jnp.mean(total * total, axis=1, keepdims=True) + EPSILON)
-    gain = gain_ref[...]
-    mine = jnp.where(h == 0, total[:, :half], total[:, half:])
+    for piece in range(2):
+        swap(piece).wait_recv()
+
+    def joined(piece):
+        here = slice(piece * half, (piece + 1) * half)
+        both = attn_buf[piece].astype(f32) + attn_in[piece].astype(f32)
+        return hidden_ref[:, here].astype(f32) + both
+
+    sums = [joined(0), joined(1)]
+    square = sums[0] * sums[0] + sums[1] * sums[1]
+    inverse = lax.rsqrt(jnp.sum(square, axis=1, keepdims=True) / cols + EPSILON)
+    mine = jnp.where(h == 0, sums[0], sums[1])
     mixed[...] = mine
+    gain = ffn_gain_ref[...]
     own_gain = jnp.where(h == 0, gain[:, :half], gain[:, half:])
     x_buf[z] = (mine * inverse * own_gain).astype(bf16)
 
@@ -467,14 +594,16 @@
         for step in (3, 1, 2):
             go(k, step).start()
         rows_in[k, h, c] = stage[k, c]
+        share(k, 0).start()
 
     def meet_rows(k):
         for step in (1, 2, 3):
             go_in(k, step).wait_recv()
-        share(k).start()
+            share(k, step).start()
 
     def work(k):
-        share_in(k).wait_recv()
+        for step in range(4):
+            share_in(k, step).wait_recv()
         rows = jnp.concatenate(
             [rows_in[k, 0].reshape(four, half), rows_in[k, 1].reshape(four, half)], axis=1
         )
@@ -508,32 +637,54 @@
             ret_back(k, step).wait_recv()
         return jnp.dot(place_buf[k], ret_in[k].reshape(four, half), preferred_element_type=f32)
 
+    def decode_rows():
+        shape = (DEC_SLOTS * BLOCK, slot_ref.shape[1])
+        wanted = (2 * s + h) * DEC_SLOTS + lax.div(iota(shape, 0), BLOCK)
+        named = one_hot(slot_ref[...] == wanted)
+        span = keys_buf.shape[0] * tok_rows
+        shape = (slot_ref.shape[1], span)
+        spread = one_hot(lax.div(iota(shape, 1), BLOCK) == iota(shape, 0))
+        blocks = jnp.dot(named, spread, preferred_element_type=f32)
+        shape = (DEC_SLOTS * BLOCK, span)
+        same = lax.rem(iota(shape, 1), BLOCK) == lax.rem(iota(shape, 0), BLOCK)
+        picked = one_hot(same & (blocks > 0.0))
+        return jnp.dot(
+            picked, keys_buf[...].reshape(span, keys_buf.shape[3]), preferred_element_type=f32
+        ).astype(bf16)
+
     @pl.loop(0, 6)
     def _(t):
-        @pl.when(t >= 3)
-        def _():
-            send_back(t - 2)
-
         @pl.when(t <= 3)
         def _():
             ring(t)
             pick(t)
 
-        @pl.when(t <= 2)
-        def _():
-            prepare(t + 1)
+        @pl.when(t == 0)
+        def _():
+            @pl.loop(1, 4)
+            def _(k):
+                prepare(k)
 
         @pl.when(t == 1)
         def _():
-            for load in loads:
-                load.wait()
+            loads[4].wait()
+            loads[5].wait()
 
         @pl.when((t >= 1) & (t <= 4))
         def _():
             meet_rows(t - 1)
+
+        @pl.when(t >= 3)
+        def _():
+            send_back(t - 2)
+
+        @pl.when((t >= 1) & (t <= 4))
+        def _():
             work(t - 1)
 
     send_back(0)
+
+    decode_ref[...] = decode_rows()
 
     @pl.loop(1, 4)
     def _(k):
@@ -545,7 +696,8 @@
         home_in(back).wait_recv()
         result = result + z_in[lax.rem(z + back, 4)].astype(f32)
     out_ref[...] = result.astype(out_ref.dtype)
-    swap.wait_send()
+    for piece in range(2):
+        swap(piece).wait_send()
 
     @pl.loop(0, 4)
     def _(k):
@@ -560,31 +712,84 @@
         for step in (1, 2, 3):
             go(k, step).wait_send()
             ret(k, step).wait_send()
-        share(k).wait_send()
+        for step in range(4):
+            share(k, step).wait_send()
         part(k).wait_send()
 
         @pl.when(k > 0)
         def _():
             home(k).wait_send()
 
-
-def expert_layer(hidden, attn_part, tail, ffn_gain, router, gate_up, down):
+    @pl.loop(0, 4)
+    def _(k):
+        @pl.when((k <= z) & (z < 3))
+        def _():
+            key_up_move(k).wait_send()
+
+        @pl.when((k <= 3 - z) & (z > 0))
+        def _():
+            key_low_move(k).wait_send()
+
+        for step in (1, 2, 3):
+            plane(k, step).wait_send()
+        share_keys(k).wait_send()
+
+
+def layer(
+    req_len,
+    req_offset,
+    hidden,
+    attn_gain,
+    kv_down,
+    kv_gain,
+    expert_ids,
+    decode_slot,
+    ffn_gain,
+    router,
+    queries,
+    key_up,
+    value_up,
+    out_proj,
+    gate_up,
+    down,
+    seq_count,
+):
     tok_rows, cols = hidden.shape
     half = cols // 2
-    expert_count = router.shape[1]
-    slots = max(2, tok_rows * TOP * 4 // (3 * expert_count))
+    heads = key_up.shape[0]
+    width = KV_RANK + 128
+    slots = max(2, tok_rows * TOP * 4 // (3 * router.shape[1]))
+    lanes = np.arange(128) % (ROPE // 2)
+    frequency = np.exp(-math.log(ROPE_BASE) * lanes * (2.0 / ROPE)).astype(np.float32)[None, :]
+    bf16, f32 = jnp.bfloat16, jnp.float32
     vmem = pl.BlockSpec(memory_space=pltpu.VMEM)
+    smem = pl.BlockSpec(memory_space=pltpu.SMEM)
     hbm = pl.BlockSpec(memory_space=pl.ANY)
     dma = pltpu.SemaphoreType.DMA
-    bf16, f32 = jnp.bfloat16, jnp.float32
-    sizes = [2, 2] + [4] * 4 + [12] * 2 + [4] * 4 + [12] * 2 + [4] * 2
+    part_rows = heads * tok_rows // 2
+    sizes = [6] + [4] * 4 + [12] * 2 + [4] * 2 + [2] * 2
+    sizes += [4] * 4 + [12] * 2 + [16] * 2 + [4] * 2 + [12] * 2 + [4] * 2
     return pl.pallas_call(
-        expert_kernel,
-        out_shape=jax.ShapeDtypeStruct((tok_rows, half), bf16),
-        in_specs=[vmem] * 5 + [hbm] * 2,
-        out_specs=vmem,
+        layer_kernel,
+        out_shape=(
+            jax.ShapeDtypeStruct((tok_rows, half), bf16),
+            jax.ShapeDtypeStruct((DEC_SLOTS * BLOCK, width), bf16),
+        ),
+        in_specs=[smem] * 2 + [vmem] * 9 + [hbm] * 6,
+        out_specs=(vmem, vmem),
         scratch_shapes=[
-            pltpu.VMEM((tok_rows, cols), bf16),
+            pltpu.VMEM((seq_count, 2, tok_rows // 2, width), bf16),
+            pltpu.VMEM(queries.shape, bf16),
+            pltpu.VMEM(key_up.shape, bf16),
+            pltpu.VMEM(value_up.shape, bf16),
+            pltpu.VMEM(out_proj.shape, bf16),
+            pltpu.VMEM((heads * tok_rows, width), bf16),
+            pltpu.VMEM((2, part_rows, KV_RANK), f32),
+            pltpu.VMEM((2, part_rows, 128), f32),
+            pltpu.VMEM((2, part_rows, 128), f32),
+            pltpu.VMEM((tok_rows, heads * V_HEAD), bf16),
+            pltpu.VMEM((2, tok_rows, half), bf16),
+            pltpu.VMEM((2, tok_rows, half), bf16),
             pltpu.VMEM((tok_rows, half), f32),
             pltpu.VMEM((4, tok_rows, half), bf16),
             pltpu.VMEM((4, 4, slots, half), bf16),
@@ -603,112 +808,27 @@
         ]
         + [dma((size,)) for size in sizes],
         compiler_params=pltpu.CompilerParams(
-            collective_id=1, has_side_effects=True, vmem_limit_bytes=56 * 1024 * 1024
+            collective_id=0, has_side_effects=True, vmem_limit_bytes=60 * 1024 * 1024
         ),
-    )(hidden, attn_part, ffn_gain[None, :], tail, router.T, gate_up, down)
-
-
-def attend_kernel(
-    key_tile,
-    span_ref,
-    first_ref,
-    nope_ref,
-    rope_ref,
-    keys_ref,
-    key_up_ref,
-    value_up_ref,
-    out_proj_ref,
-    out_ref,
-    query,
-    acc,
-    peak,
-    total,
-    heads_buf,
-):
-    heads, tok_rows = nope_ref.shape[0], nope_ref.shape[1]
-    group = 4
-    group_rows = group * tok_rows
-    score_scale = 1.0 / math.sqrt(NOPE + ROPE)
-    contract = (((1,), (1,)), ((), ()))
-    for head in range(heads):
-        here = slice(head * tok_rows, (head + 1) * tok_rows)
-        query[here, :KV_RANK] = jnp.dot(
-            nope_ref[head], key_up_ref[head], preferred_element_type=jnp.float32
-        ).astype(jnp.bfloat16)
-        query[here, KV_RANK:] = rope_ref[head]
-    first = jnp.concatenate([first_ref[...]] * group, axis=0)
-    own = span_ref[2] + lax.broadcasted_iota(jnp.int32, (tok_rows, 1), 0)
-    own = jnp.concatenate([own] * group, axis=0)
-
-    @pl.loop(0, heads // group)
-    def _(part_no):
-        base = pl.multiple_of(part_no * group_rows, group_rows)
-        here = pl.ds(base, group_rows)
-        peak[...] = jnp.full_like(peak, MASKED)
-        total[...] = jnp.zeros_like(total)
-        acc[...] = jnp.zeros_like(acc)
-
-        @pl.loop(span_ref[0], span_ref[1])
-        def _(tile):
-            start = pl.multiple_of(tile * key_tile, key_tile)
-            keys = keys_ref[pl.ds(start, key_tile), :]
-            scores = score_scale * lax.dot_general(
-                query[here, :], keys, contract, preferred_element_type=jnp.float32
-            )
-            index = start + lax.broadcasted_iota(jnp.int32, scores.shape, 1)
-            allowed = (index <= own) & (index >= first)
-            scores = jnp.where(allowed, scores, MASKED)
-            old = peak[:, :1]
-            new = jnp.maximum(old, jnp.max(scores, axis=1, keepdims=True))
-            terms = jnp.where(allowed, jnp.exp(scores - new), 0.0)
-            fade = jnp.exp(old - new)
-            total[:, :1] = total[:, :1] * fade + jnp.sum(terms, axis=1, keepdims=True)
-            peak[:, :1] = new
-            acc[...] = acc[...] * fade + jnp.dot(
-                terms.astype(jnp.bfloat16), keys[:, :KV_RANK], preferred_element_type=jnp.float32
-            )
-
-        attended = (acc[...] / total[:, :1]).astype(jnp.bfloat16)
-        for member in range(group):
-            heads_buf[part_no * group + member] = jnp.dot(
-                attended[member * tok_rows : (member + 1) * tok_rows],
-                value_up_ref[part_no * group + member],
-                preferred_element_type=jnp.float32,
-            ).astype(jnp.bfloat16)
-
-    joined = jnp.concatenate([heads_buf[head] for head in range(heads)], axis=1)
-    out_ref[...] = jnp.dot(
-        joined, out_proj_ref[...], preferred_element_type=jnp.float32
-    ).astype(out_ref.dtype)
-
-
-def attend_rows(nope, rope, keys, key_up, value_up, out_proj, first, first_token):
-    heads, tok_rows = nope.shape[0], nope.shape[1]
-    key_tile = 512 if keys.shape[0] % 512 == 0 else 128
-    width = keys.shape[1]
-    span = jnp.stack(
-        [
-            jnp.min(first) // key_tile,
-            (first_token + tok_rows + key_tile - 1) // key_tile,
-            first_token,
-        ]
-    ).astype(jnp.int32)
-    vmem = pl.BlockSpec(memory_space=pltpu.VMEM)
-    rows = 4 * tok_rows
-    return pl.pallas_call(
-        functools.partial(attend_kernel, key_tile),
-        out_shape=jax.ShapeDtypeStruct((tok_rows, out_proj.shape[1]), jnp.bfloat16),
-        in_specs=[pl.BlockSpec(memory_space=pltpu.SMEM)] + [vmem] * 7,
-        out_specs=vmem,
-        scratch_shapes=[
-            pltpu.VMEM((heads * tok_rows, width), jnp.bfloat16),
-            pltpu.VMEM((rows, KV_RANK), jnp.float32),
-            pltpu.VMEM((rows, 128), jnp.float32),
-            pltpu.VMEM((rows, 128), jnp.float32),
-            pltpu.VMEM((heads, tok_rows, V_HEAD), jnp.bfloat16),
-        ],
-        compiler_params=pltpu.CompilerParams(vmem_limit_bytes=40 * 1024 * 1024),
-    )(span, first[:, None], nope, rope, keys, key_up, value_up, out_proj)
+    )(
+        req_len,
+        req_offset,
+        jnp.asarray(frequency),
+        hidden,
+        attn_gain[None, :],
+        kv_down.T,
+        kv_gain[None, :],
+        expert_ids.T,
+        decode_slot[None, :],
+        ffn_gain[None, :],
+        router.T,
+        queries,
+        key_up,
+        value_up,
+        out_proj,
+        gate_up,
+        down,
+    )
 
 
 def body(
@@ -766,44 +886,27 @@
     seq_count = lax.axis_size("seq")
     fast = seq_count == 16 and head_count == 2 and expert_count == 16
     if fast:
-        route_mask = jnp.any(expert_ids[:, :, None] == expert_axis[None, None, :], axis=1)
-        payload = jnp.concatenate([latent, key_rope, route_mask.astype(jnp.bfloat16)], axis=1)
-        payload = jnp.pad(payload, ((0, 0), (0, -payload.shape[1] % 128)))
-        gathered = gather_rows(payload, seq_count)
-        by_head = jnp.swapaxes(head_view, 0, 1)
-        rope_pad = gathered.shape[1] - KV_RANK - ROPE
-        by_head_rope = jnp.pad(jnp.swapaxes(query_rope, 0, 1), ((0, 0), (0, 0), (0, rope_pad)))
-        req_ends = running(req_len)
-        member = my_request[:, None] == jnp.arange(req_len.shape[0])[None, :]
-        first = jnp.sum(jnp.where(member, (req_ends - req_len)[None, :], 0), axis=1)
-        attn_part = attend_rows(
-            by_head[:, :, :NOPE],
-            by_head_rope,
-            gathered,
+        output, slot_rows = layer(
+            req_len,
+            req_offset,
+            hidden,
+            attn_gain,
+            kv_down,
+            kv_gain,
+            expert_ids,
+            decode_slot,
+            ffn_gain,
+            router,
+            queries,
             key_up,
             value_up,
             out_proj,
-            first,
-            seq_place * tok_rows,
-        )
-        source_row = source_block[:, None] * BLOCK + jnp.arange(BLOCK, dtype=jnp.int32)[None, :]
-        pick_rows = source_row[:, :, None] == jnp.arange(gathered.shape[0], dtype=jnp.int32)
-        pick_rows = (pick_rows & slot_filled[:, None, None]).reshape(DEC_SLOTS * BLOCK, -1)
-        slot_rows = jnp.dot(
-            pick_rows.astype(jnp.bfloat16), gathered, preferred_element_type=jnp.float32
-        ).astype(jnp.bfloat16)
+            jnp.swapaxes(expert_gate_up[0], 1, 2),
+            expert_down[0],
+            seq_count,
+        )
         decode_latent = slot_rows[:, :KV_RANK].reshape(DEC_SLOTS, BLOCK, KV_RANK)
         decode_rope = slot_rows[:, KV_RANK : KV_RANK + ROPE].reshape(DEC_SLOTS, BLOCK * ROPE)
-        tail = gathered[:, KV_RANK : KV_RANK + 128].reshape(seq_count, tok_rows, 128)
-        output = expert_layer(
-            hidden,
-            attn_part,
-            tail,
-            ffn_gain,
-            router,
-            jnp.swapaxes(expert_gate_up[0], 1, 2),
-            expert_down[0],
-        )
         return (output, decode_latent, decode_rope)
     else:
         piece_latent = lax.all_gather(latent, "seq", axis=0, tiled=True)

time: 141 us -> 105 us (0.74)
  Pallas kernels: 113 us -> 100 us
  other arithmetic: 9.6 us -> 0 us
  local copies, waits for them, and re-layouts: 11.9 us -> 4.55 us
  between operations: 3.46 us -> 0.65 us
  matrix products: 2.51 us -> 0 us
    pallas_call x3 -> x1, Pallas kernels: 113 us -> 100 us  [layer(): pl.pallas_call(layer_kernel, out_shape=(jax.ShapeDtypeStruct((tok_rows, h...]
    reduce_sum x6 -> x0, other arithmetic: 3.93 us -> none  [the longest x2 1.31 us: rms_rows(): jnp.mean(values * values, axis=-1, keepdims=True) + EPSILON]
    slice x2 -> x0, local copies, waits for them, and re-layouts: 2.6 us -> none  [the longest x1 1.76 us: body(): by_head[:, :, :NOPE]]
    dot_general x2 -> x0, matrix products: 2.51 us -> none  [the longest x1 1.89 us: body(): kv_full = jnp.dot(normed, kv_down, preferred_element_type=jnp.float32)]
    convert_element_type x1 -> x0, local copies, waits for them, and re-layouts: 1.92 us -> none  [rotate(): first_half = values[..., :half_width].astype(jnp.float32)]
    another operation x3 -> x0, other arithmetic: 1.76 us -> none
    reduce_or x2 -> x0, other arithmetic: 1.54 us -> none  [the longest x1 0.84 us: body(): slot_filled = jnp.any(slot_match, axis=1)]
    unnamed x21 -> x1, local copies, waits for them, and re-layouts: 3.15 us -> 1.67 us
where the time goes in v3:
time: 105 us
  Pallas kernels  100 us (95%)
  local copies, waits for them, and re-layouts  4.55 us (4%)
    pallas_call x1, Pallas kernels, layer(): pl.pallas_call(layer_kernel, out_shape=(jax.ShapeDtypeStruct((tok_rows, h...  100 us

profile of v3, /device:TPU:0, one launch (start us, length us, event | category | flops | bytes accessed | tf_op | source)
XLA Modules:
  0.0 105.2 jit_solution(11541526540955612587)
XLA Ops:
  0.6 100.0 %shard_map.184 = (bf16[128,1024]{1,0:T(8,128)(2,1)}, bf16[64,640]{1,0:T(8,128)(2,1)}) custom-call(s32[2]{0:T(128)} %req_len_ref.1, s32[2]{0:T(128)} %req_offset_ref.1, f32[1,128]{1,0:T(1,128)} %constant.2.clone.freq_ref, bf16[128,2048]{1,0:T(8,128)(2,1)} %hidden_ref.1, f32[1,2048]{1,0:T(1,128)} %bitcast.17, bf16[576,2048]{1,0:T(8,128)(2,1)} %bitcast.14, ...), custom_call_target="tpu_custom_call" | custom-call | tf_op jit(solution)/shard_map/pallas_call | solution.py:772
  100.6 1.5 %slice.6 = bf16[64,512]{1,0:T(8,128)(2,1)} slice(bf16[64,640]{1,0:T(8,128)(2,1)} %get-tuple-element.6), slice={[0:64], [0:512]} | slice | bytes 131072 | tf_op jit(solution)/shard_map/slice | solution.py:908
  102.1 0.7 slice.7
  102.8 0.7 reshape.13
  103.5 1.7 %copy.21 = bf16[128,1024]{1,0:T(8,128)(2,1)} copy(bf16[128,1024]{1,0:T(8,128)(2,1)} %get-tuple-element.10) | data formatting | bytes 524288

commit v4 on v3

--- a/solution.py
+++ b/solution.py
@@ -23,6 +23,7 @@
 ROUTE_SCALE = 2.446
 EPSILON = 1e-06
 MASKED = -1e30
+PIECES = 2
 
 
 def rms_rows(values, scale_gain):
@@ -119,12 +120,12 @@
     freq_ref,
     hidden_ref,
     gain_ref,
-    kv_ref,
     kv_gain_ref,
     ids_ref,
     slot_ref,
     ffn_gain_ref,
     router_ref,
+    kv_hbm,
     queries_hbm,
     key_up_hbm,
     value_up_hbm,
@@ -132,7 +133,9 @@
     gate_up_hbm,
     down_hbm,
     out_ref,
-    decode_ref,
+    latent_ref,
+    rope_ref,
+    kv_buf,
     keys_buf,
     queries,
     key_up,
@@ -200,9 +203,10 @@
     pairs = [(queries_hbm, queries), (key_up_hbm, key_up)]
     pairs += [(value_up_hbm, value_up), (out_proj_hbm, out_proj)]
     pairs += [(gate_up_hbm, gate_up), (down_hbm, down)]
+    pairs += [(kv_hbm, kv_buf)]
     loads = [pltpu.make_async_copy(*both, load_sem.at[i]) for i, both in enumerate(pairs)]
-    for load in loads:
-        load.start()
+    for index in (6, 0, 1):
+        loads[index].start()
 
     barrier = pltpu.get_barrier_semaphore()
     peers = [(line_place(lax.rem(z + back, 4), s), h) for back in range(1, 4)]
@@ -296,9 +300,10 @@
     rows = hidden_ref[pl.ds(pl.multiple_of(h * rows_half, rows_half), rows_half), :].astype(f32)
     inverse = lax.rsqrt(jnp.mean(rows * rows, axis=1, keepdims=True) + EPSILON)
     normed = (rows * inverse * gain_ref[...]).astype(bf16)
-    full = lax.dot_general(normed, kv_ref[:KV_RANK], pair, preferred_element_type=f32)
+    loads[6].wait()
+    full = lax.dot_general(normed, kv_buf[:KV_RANK], pair, preferred_element_type=f32)
     end = lax.dot_general(
-        normed, kv_ref[KV_RANK + ROPE - 128 :], pair, preferred_element_type=f32
+        normed, kv_buf[KV_RANK + ROPE - 128 :], pair, preferred_element_type=f32
     )
     inverse = lax.rsqrt(jnp.mean(full * full, axis=1, keepdims=True) + EPSILON)
     keys_buf[s, h, :, :KV_RANK] = (full * inverse * kv_gain_ref[...]).astype(bf16)
@@ -340,8 +345,11 @@
         share_keys(k).start()
 
     key_ring(0)
+    for index in range(2, 6):
+        loads[index].start()
     token = base + iota((tok_rows, 1), 0)
-    turn = turns(token)
+    scale = math.log2(math.e) / math.sqrt(NOPE + ROPE)
+    turn = [scale * part for part in turns(token)]
     loads[0].wait()
     loads[1].wait()
     for two in range(heads // 2):
@@ -354,50 +362,52 @@
         for odd, columns, rotary in ((0, left, middle), (1, nope, turned)):
             head = 2 * two + odd
             here = slice(head * tok_rows, (head + 1) * tok_rows)
-            query[here, :KV_RANK] = jnp.dot(
-                columns, key_up[head], preferred_element_type=f32
-            ).astype(bf16)
+            latent = jnp.dot(columns, key_up[head], preferred_element_type=f32)
+            query[here, :KV_RANK] = (scale * latent).astype(bf16)
             query[here, KV_RANK:] = spin(rotary, turn)
-    peak[...] = jnp.full_like(peak, MASKED)
-    total[...] = jnp.zeros_like(total)
-    acc[...] = jnp.zeros_like(acc)
     first = jnp.concatenate([starts_of(token)[0]] * part_heads, axis=0)
     own = jnp.concatenate([token] * part_heads, axis=0)
-    scale = math.log2(math.e) / math.sqrt(NOPE + ROPE)
-
-    def attend(k, part_no):
+    def attend(k, part_no, leading=False):
         line = line_of(k)
         keys = keys_buf[pl.ds(line * 4, 4)].reshape(tile_keys, keys_buf.shape[3])
         here = slice(part_no * part_rows, (part_no + 1) * part_rows)
-        scores = scale * lax.dot_general(query[here, :], keys, pair, preferred_element_type=f32)
+        scores = lax.dot_general(query[here, :], keys, pair, preferred_element_type=f32)
         index = line * tile_keys + iota(scores.shape, 1)
-        scores = jnp.where((index <= own) & (index >= first), scores, MASKED)
-        old = peak[part_no, :, :1]
-        new = jnp.maximum(old, jnp.max(scores, axis=1, keepdims=True))
+        allowed = index >= first
+        if leading:
+            allowed = allowed & (index <= own)
+        scores = jnp.where(allowed, scores, MASKED)
+        new = jnp.max(scores, axis=1, keepdims=True)
+        if not leading:
+            old = peak[part_no, :, :1]
+            new = jnp.maximum(old, new)
+            fade = jnp.exp2(old - new)
         terms = jnp.exp2(scores - new)
-        fade = jnp.exp2(old - new)
-        total[part_no, :, :1] = total[part_no, :, :1] * fade + jnp.sum(
-            terms, axis=1, keepdims=True
-        )
+        norm = jnp.sum(terms, axis=1, keepdims=True)
+        mixture = jnp.dot(terms.astype(bf16), keys[:, :KV_RANK], preferred_element_type=f32)
+        if not leading:
+            norm = total[part_no, :, :1] * fade + norm
+            mixture = acc[part_no] * fade + mixture
         peak[part_no, :, :1] = new
-        acc[part_no] = acc[part_no] * fade + jnp.dot(
-            terms.astype(bf16), keys[:, :KV_RANK], preferred_element_type=f32
-        )
+        total[part_no, :, :1] = norm
+        acc[part_no] = mixture
 
     key_ring(1)
     meet_keys(0)
-
-    @pl.loop(0, 4)
+    key_ring(2)
+    share_keys_in(0).wait_recv()
+    attend(0, 0, True)
+    key_ring(3)
+    meet_keys(1)
+    attend(0, 1, True)
+
+    @pl.loop(1, 4)
     def _(k):
         share_keys_in(k).wait_recv()
 
         @pl.when(k <= z)
         def _():
             attend(k, 0)
-
-        @pl.when(k <= 1)
-        def _():
-            key_ring(k + 2)
 
         @pl.when(k <= 2)
         def _():
@@ -434,38 +444,45 @@
             heads_buf[...], out_proj[:, here], preferred_element_type=f32
         ).astype(bf16)
         swap(piece).start()
-    def up(t):
-        view = x_buf.at[z - t]
+    def part_of(q):
+        return pl.ds(q * (half // PIECES), half // PIECES)
+
+    def up(t, q):
+        view = x_buf.at[z - t, :, part_of(q)]
         device = (line_place(lax.rem(z + 1, 4), s), h)
-        return remote(view, view, up_send.at[t], up_recv.at[t], device)
-
-    def up_in(t):
-        view = x_buf.at[z - t]
-        return remote(view, view, up_send.at[t - 1], up_recv.at[t - 1], sibling)
-
-    def low(t):
-        view = x_buf.at[z + t]
+        index = PIECES * t + q
+        return remote(view, view, up_send.at[index], up_recv.at[index], device)
+
+    def up_in(t, q):
+        view = x_buf.at[z - t, :, part_of(q)]
+        index = PIECES * (t - 1) + q
+        return remote(view, view, up_send.at[index], up_recv.at[index], sibling)
+
+    def low(t, q):
+        view = x_buf.at[z + t, :, part_of(q)]
         device = (line_place(lax.rem(z + 3, 4), s), h)
-        return remote(view, view, down_send.at[t], down_recv.at[t], device)
-
-    def low_in(t):
-        view = x_buf.at[z + t]
-        return remote(view, view, down_send.at[t - 1], down_recv.at[t - 1], sibling)
-
-    def go(k, step):
+        index = PIECES * t + q
+        return remote(view, view, down_send.at[index], down_recv.at[index], device)
+
+    def low_in(t, q):
+        view = x_buf.at[z + t, :, part_of(q)]
+        index = PIECES * (t - 1) + q
+        return remote(view, view, down_send.at[index], down_recv.at[index], sibling)
+
+    def go(k, step, q):
         other = across(s, step)
-        index = 3 * k + step - 1
+        index = PIECES * (3 * k + step - 1) + q
         return remote(
-            stage.at[k, lax.rem(other, 4)],
-            rows_in.at[k, h, c],
+            stage.at[k, lax.rem(other, 4), :, part_of(q)],
+            rows_in.at[k, h, c, :, part_of(q)],
             go_send.at[index],
             go_recv.at[index],
             (other, h),
         )
 
-    def go_in(k, step):
-        index = 3 * k + step - 1
-        view = rows_in.at[k, h, lax.rem(across(s, step), 4)]
+    def go_in(k, step, q):
+        index = PIECES * (3 * k + step - 1) + q
+        view = rows_in.at[k, h, lax.rem(across(s, step), 4), :, part_of(q)]
         return remote(view, view, go_send.at[index], go_recv.at[index], sibling)
 
     def share(k, step):
@@ -481,29 +498,36 @@
     def part(k):
         return remote(res.at[k, 1 - h], sib_in.at[k], part_send.at[k], part_recv.at[k], sibling)
 
-    def ret(k, step):
+    def ret(k, step, q):
         other = across(s, step)
-        index = 3 * k + step - 1
+        index = PIECES * (3 * k + step - 1) + q
         return remote(
-            res.at[k, h, lax.rem(other, 4)],
-            ret_in.at[k, c],
+            res.at[k, h, lax.rem(other, 4), :, part_of(q)],
+            ret_in.at[k, c, :, part_of(q)],
             ret_send.at[index],
             ret_recv.at[index],
             (other, h),
         )
 
-    def ret_back(k, step):
-        index = 3 * k + step - 1
-        view = ret_in.at[k, lax.rem(across(s, step), 4)]
+    def ret_back(k, step, q):
+        index = PIECES * (3 * k + step - 1) + q
+        view = ret_in.at[k, lax.rem(across(s, step), 4), :, part_of(q)]
         return remote(view, view, ret_send.at[index], ret_recv.at[index], sibling)
 
-    def home(k):
+    def home(k, q):
         owner = (line_place(turn_line(z, k), s), h)
-        return remote(z_out.at[k], z_in.at[z], home_send.at[k], home_recv.at[z], owner)
-
-    def home_in(back):
+        return remote(
+            z_out.at[k, :, part_of(q)],
+            z_in.at[z, :, part_of(q)],
+            home_send.at[PIECES * k + q],
+            home_recv.at[PIECES * z + q],
+            owner,
+        )
+
+    def home_in(back, q):
         line = lax.rem(z + back, 4)
-        return remote(z_in.at[line], z_in.at[line], home_send.at[0], home_recv.at[line], sibling)
+        view = z_in.at[line, :, part_of(q)]
+        return remote(view, view, home_send.at[q], home_recv.at[PIECES * line + q], sibling)
 
     slots = stage.shape[2]
     expert_count = router_ref.shape[0]
@@ -571,34 +595,38 @@
     own_gain = jnp.where(h == 0, gain[:, :half], gain[:, half:])
     x_buf[z] = (mine * inverse * own_gain).astype(bf16)
 
-    def ring(t):
+    def ring(t, q):
         @pl.when((t >= 1) & (t <= z))
         def _():
-            up_in(t).wait_recv()
+            up_in(t, q).wait_recv()
 
         @pl.when((t <= z) & (z < 3))
         def _():
-            up(t).start()
+            up(t, q).start()
 
         @pl.when((t >= 1) & (t <= 3 - z))
         def _():
-            low_in(t).wait_recv()
+            low_in(t, q).wait_recv()
 
         @pl.when((t <= 3 - z) & (z > 0))
         def _():
-            low(t).start()
-
-    def pick(k):
-        rows = jnp.dot(pick_buf[k], x_buf[turn_line(z, k)], preferred_element_type=f32)
-        stage[k] = rows.astype(bf16).reshape(4, slots, half)
+            low(t, q).start()
+
+    def pick(k, q):
+        here = part_of(q)
+        rows = jnp.dot(
+            pick_buf[k], x_buf[turn_line(z, k), :, here], preferred_element_type=f32
+        )
+        stage[k, :, :, here] = rows.astype(bf16).reshape(4, slots, half // PIECES)
         for step in (3, 1, 2):
-            go(k, step).start()
-        rows_in[k, h, c] = stage[k, c]
+            go(k, step, q).start()
+        rows_in[k, h, c, :, here] = stage[k, c, :, here]
+
+    def meet_rows(k):
         share(k, 0).start()
-
-    def meet_rows(k):
         for step in (1, 2, 3):
-            go_in(k, step).wait_recv()
+            for q in range(PIECES):
+                go_in(k, step, q).wait_recv()
             share(k, step).start()
 
     def work(k):
@@ -620,44 +648,72 @@
         gate = lax.dot_general(rows, gate_up[0], pair, preferred_element_type=f32)
         rise = lax.dot_general(rows, gate_up[1], pair, preferred_element_type=f32)
         act = (gate / (1.0 + jnp.exp(-gate)) * rise * weight).astype(bf16)
-        out = jnp.dot(act, down[...], preferred_element_type=f32).astype(bf16)
-        res[k, 0] = out[:, :half].reshape(4, slots, half)
-        res[k, 1] = out[:, half:].reshape(4, slots, half)
-        part(k).start()
+        for owner in (1 - h, h):
+            here = pl.ds(pl.multiple_of(owner * half, half), half)
+            out = jnp.dot(act, down[:, here], preferred_element_type=f32).astype(bf16)
+            res[k, owner] = out.reshape(4, slots, half)
+            if owner is not h:
+                part(k).start()
 
     def send_back(k):
         part(k).wait_recv()
-        res[k, h] = (res[k, h].astype(f32) + sib_in[k].astype(f32)).astype(bf16)
-        for step in (3, 1, 2):
-            ret(k, step).start()
-        ret_in[k, c] = res[k, h, c]
-
-    def place(k):
+        for q in range(PIECES):
+            here = part_of(q)
+            both = res[k, h, :, :, here].astype(f32) + sib_in[k, :, :, here].astype(f32)
+            res[k, h, :, :, here] = both.astype(bf16)
+            for step in (3, 1, 2):
+                ret(k, step, q).start()
+            ret_in[k, c, :, here] = res[k, h, c, :, here]
+
+    def place(k, q):
         for step in (1, 2, 3):
-            ret_back(k, step).wait_recv()
-        return jnp.dot(place_buf[k], ret_in[k].reshape(four, half), preferred_element_type=f32)
+            ret_back(k, step, q).wait_recv()
+        rows = ret_in[k, :, :, part_of(q)].reshape(four, half // PIECES)
+        return jnp.dot(place_buf[k], rows, preferred_element_type=f32)
+
+    def go_home(k):
+        for q in range(PIECES):
+            z_out[k, :, part_of(q)] = place(k, q).astype(bf16)
+            home(k, q).start()
 
     def decode_rows():
-        shape = (DEC_SLOTS * BLOCK, slot_ref.shape[1])
-        wanted = (2 * s + h) * DEC_SLOTS + lax.div(iota(shape, 0), BLOCK)
-        named = one_hot(slot_ref[...] == wanted)
         span = keys_buf.shape[0] * tok_rows
+        keys = keys_buf[...].reshape(span, keys_buf.shape[3])
         shape = (slot_ref.shape[1], span)
         spread = one_hot(lax.div(iota(shape, 1), BLOCK) == iota(shape, 0))
-        blocks = jnp.dot(named, spread, preferred_element_type=f32)
-        shape = (DEC_SLOTS * BLOCK, span)
-        same = lax.rem(iota(shape, 1), BLOCK) == lax.rem(iota(shape, 0), BLOCK)
-        picked = one_hot(same & (blocks > 0.0))
-        return jnp.dot(
-            picked, keys_buf[...].reshape(span, keys_buf.shape[3]), preferred_element_type=f32
-        ).astype(bf16)
+        device_slot = (2 * s + h) * DEC_SLOTS
+
+        def rows_of(slot, row, values):
+            named = one_hot(slot_ref[...] == slot)
+            blocks = jnp.dot(named, spread, preferred_element_type=f32)
+            same = lax.rem(iota(blocks.shape, 1), BLOCK) == row
+            picked = one_hot(same & (blocks > 0.0))
+            return jnp.dot(picked, values, preferred_element_type=f32)
+
+        place = iota((DEC_SLOTS * BLOCK, 1), 0)
+        latent = rows_of(
+            device_slot + lax.div(place, BLOCK), lax.rem(place, BLOCK), keys[:, :KV_RANK]
+        )
+        latent_ref[...] = latent.astype(bf16)
+        place = iota((8 * BLOCK, 1), 0)
+        slot = lax.rem(place, 8)
+        slot = jnp.where(slot < DEC_SLOTS, device_slot + slot, -1)
+        rope = rows_of(slot, lax.div(place, 8), keys[:, KV_RANK:])
+        pieces = []
+        for two in range(BLOCK // 2):
+            left = rope[16 * two : 16 * two + 8]
+            right = pltpu.roll(rope[16 * two + 8 : 16 * two + 16], ROPE, 1)
+            pieces.append(jnp.where(iota(left.shape, 1) < ROPE, left, right))
+        flat = jnp.concatenate(pieces, axis=1)
+        rope_ref[...] = flat[:DEC_SLOTS].astype(bf16)
 
     @pl.loop(0, 6)
     def _(t):
         @pl.when(t <= 3)
         def _():
-            ring(t)
-            pick(t)
+            for q in range(PIECES):
+                ring(t, q)
+                pick(t, q)
 
         @pl.when(t == 0)
         def _():
@@ -682,43 +738,51 @@
         def _():
             work(t - 1)
 
+        @pl.when(t == 4)
+        def _():
+            go_home(1)
+
+    @pl.loop(2, 4)
+    def _(k):
+        go_home(k)
+
     send_back(0)
-
-    decode_ref[...] = decode_rows()
-
-    @pl.loop(1, 4)
-    def _(k):
-        z_out[k] = place(k).astype(bf16)
-        home(k).start()
-
-    result = mixed[...] + place(0)
-    for back in (1, 2, 3):
-        home_in(back).wait_recv()
-        result = result + z_in[lax.rem(z + back, 4)].astype(f32)
-    out_ref[...] = result.astype(out_ref.dtype)
+    decode_rows()
+    for q in range(PIECES):
+        here = part_of(q)
+        mixed[:, here] = mixed[:, here] + place(0, q)
+    for q in range(PIECES):
+        here = part_of(q)
+        result = mixed[:, here]
+        for back in (1, 2, 3):
+            home_in(back, q).wait_recv()
+            result = result + z_in[lax.rem(z + back, 4), :, here].astype(f32)
+        out_ref[:, here] = result.astype(out_ref.dtype)
     for piece in range(2):
         swap(piece).wait_send()
 
     @pl.loop(0, 4)
     def _(k):
-        @pl.when((k <= z) & (z < 3))
-        def _():
-            up(k).wait_send()
-
-        @pl.when((k <= 3 - z) & (z > 0))
-        def _():
-            low(k).wait_send()
-
-        for step in (1, 2, 3):
-            go(k, step).wait_send()
-            ret(k, step).wait_send()
+        for q in range(PIECES):
+            @pl.when((k <= z) & (z < 3))
+            def _():
+                up(k, q).wait_send()
+
+            @pl.when((k <= 3 - z) & (z > 0))
+            def _():
+                low(k, q).wait_send()
+
+            for step in (1, 2, 3):
+                go(k, step, q).wait_send()
+                ret(k, step, q).wait_send()
+
+            @pl.when(k > 0)
+            def _():
+                home(k, q).wait_send()
+
         for step in range(4):
             share(k, step).wait_send()
         part(k).wait_send()
-
-        @pl.when(k > 0)
-        def _():
-            home(k).wait_send()
 
     @pl.loop(0, 4)
     def _(k):
@@ -767,17 +831,20 @@
     hbm = pl.BlockSpec(memory_space=pl.ANY)
     dma = pltpu.SemaphoreType.DMA
     part_rows = heads * tok_rows // 2
-    sizes = [6] + [4] * 4 + [12] * 2 + [4] * 2 + [2] * 2
-    sizes += [4] * 4 + [12] * 2 + [16] * 2 + [4] * 2 + [12] * 2 + [4] * 2
+    sizes = [7] + [4] * 4 + [12] * 2 + [4] * 2 + [2] * 2
+    sizes += [4 * PIECES] * 4 + [12 * PIECES] * 2 + [16] * 2 + [4] * 2
+    sizes += [12 * PIECES] * 2 + [4 * PIECES] * 2
     return pl.pallas_call(
         layer_kernel,
         out_shape=(
             jax.ShapeDtypeStruct((tok_rows, half), bf16),
-            jax.ShapeDtypeStruct((DEC_SLOTS * BLOCK, width), bf16),
+            jax.ShapeDtypeStruct((DEC_SLOTS * BLOCK, KV_RANK), bf16),
+            jax.ShapeDtypeStruct((DEC_SLOTS, BLOCK * ROPE), bf16),
         ),
-        in_specs=[smem] * 2 + [vmem] * 9 + [hbm] * 6,
-        out_specs=(vmem, vmem),
+        in_specs=[smem] * 2 + [vmem] * 8 + [hbm] * 7,
+        out_specs=(vmem, vmem, vmem),
         scratch_shapes=[
+            pltpu.VMEM(kv_down.shape[::-1], bf16),
             pltpu.VMEM((seq_count, 2, tok_rows // 2, width), bf16),
             pltpu.VMEM(queries.shape, bf16),
             pltpu.VMEM(key_up.shape, bf16),
@@ -816,12 +883,12 @@
         jnp.asarray(frequency),
         hidden,
         attn_gain[None, :],
-        kv_down.T,
         kv_gain[None, :],
         expert_ids.T,
         decode_slot[None, :],
         ffn_gain[None, :],
         router.T,
+        kv_down.T,
         queries,
         key_up,
         value_up,
@@ -886,7 +953,7 @@
     seq_count = lax.axis_size("seq")
     fast = seq_count == 16 and head_count == 2 and expert_count == 16
     if fast:
-        output, slot_rows = layer(
+        output, decode_latent, decode_rope = layer(
             req_len,
             req_offset,
             hidden,
@@ -905,8 +972,7 @@
             expert_down[0],
             seq_count,
         )
-        decode_latent = slot_rows[:, :KV_RANK].reshape(DEC_SLOTS, BLOCK, KV_RANK)
-        decode_rope = slot_rows[:, KV_RANK : KV_RANK + ROPE].reshape(DEC_SLOTS, BLOCK * ROPE)
+        decode_latent = decode_latent.reshape(DEC_SLOTS, BLOCK, KV_RANK)
         return (output, decode_latent, decode_rope)
     else:
         piece_latent = lax.all_gather(latent, "seq", axis=0, tiled=True)

time: 105 us -> 101 us (0.962)
  Pallas kernels: 100 us -> 95.6 us
    pallas_call x1, Pallas kernels: 100 us -> 95.6 us  [layer(): pl.pallas_call(layer_kernel, out_shape=(jax.ShapeDtypeStruct((tok_rows, h...]
    unnamed x1 -> x3, local copies, waits for them, and re-layouts: 1.67 us -> 4.44 us
    slice x2 -> x0, local copies, waits for them, and re-layouts: 2.19 us -> none  [the longest x1 1.47 us: body(): decode_latent = slot_rows[:, :KV_RANK].reshape(DEC_SLOTS, BLOCK, KV_RANK)]
where the time goes in v4:
time: 101 us
  Pallas kernels  95.6 us (95%)
  local copies, waits for them, and re-layouts  4.44 us (4%)
    pallas_call x1, Pallas kernels, layer(): pl.pallas_call(layer_kernel, out_shape=(jax.ShapeDtypeStruct((tok_rows, h...  95.6 us
    unnamed x3, local copies, waits for them, and re-layouts  4.44 us

profile of v4, /device:TPU:0, one launch (start us, length us, event | category | flops | bytes accessed | tf_op | source)
XLA Modules:
  0.0 100.7 jit_solution(4436865981991185167)
XLA Ops:
  0.6 95.6 %shard_map.184 = (bf16[128,1024]{1,0:T(8,128)(2,1)}, bf16[64,512]{1,0:T(8,128)(2,1)}, bf16[4,1024]{1,0:T(4,128)(2,1)}) custom-call(s32[2]{0:T(128)} %req_len_ref.1, s32[2]{0:T(128)} %req_offset_ref.1, f32[1,128]{1,0:T(1,128)} %constant.2.clone.freq_ref, bf16[128,2048]{1,0:T(8,128)(2,1)} %hidden_ref.1, f32[1,2048]{1,0:T(1,128)} %bitcast.17, ...), custom_call_target="tpu_custom_call" | custom-call | tf_op jit(solution)/shard_map/pallas_call | solution.py:837
  96.3 1.7 %copy.23 = bf16[128,1024]{1,0:T(8,128)(2,1)} copy(bf16[128,1024]{1,0:T(8,128)(2,1)} %get-tuple-element.12) | data formatting | bytes 524288
  97.9 1.5 %copy.24 = bf16[4,16,512]{2,1,0:T(8,128)(2,1)} copy(bf16[4,16,512]{2,1,0:T(8,128)(2,1)} %bitcast.16) | data formatting | bytes 131072
  99.4 1.3 %copy.25 = bf16[4,1024]{1,0:T(4,128)(2,1)} copy(bf16[4,1024]{1,0:T(4,128)(2,1)} %get-tuple-element.14) | data formatting | bytes 16384

commit v5 on v4

--- a/solution.py
+++ b/solution.py
@@ -188,6 +188,8 @@
     ret_recv,
     home_send,
     home_recv,
+    relay_buf,
+    relay_recv,
 ):
     s, h = lax.axis_index("seq"), lax.axis_index("head")
     z, c = lax.div(s, 4), lax.rem(s, 4)
@@ -524,11 +526,21 @@
             owner,
         )
 
-    def home_in(back, q):
-        line = lax.rem(z + back, 4)
+    def relay(k, q):
+        inner_side = (line_place(flip(z, 1), s), h)
+        return remote(
+            z_out.at[k, :, part_of(q)],
+            relay_buf.at[k - 2, :, part_of(q)],
+            home_send.at[PIECES * k + q],
+            relay_recv.at[PIECES * (k - 2) + q],
+            inner_side,
+        )
+
+    def home_in(line, q):
         view = z_in.at[line, :, part_of(q)]
         return remote(view, view, home_send.at[q], home_recv.at[PIECES * line + q], sibling)
 
+    inner = lax.rem(z + lax.div(z, 2), 2)
     slots = stage.shape[2]
     expert_count = router_ref.shape[0]
     four = 4 * slots
@@ -671,10 +683,27 @@
         rows = ret_in[k, :, :, part_of(q)].reshape(four, half // PIECES)
         return jnp.dot(place_buf[k], rows, preferred_element_type=f32)
 
-    def go_home(k):
+    def go_home(k, between=None):
+        sums = [place(k, q) for q in range(PIECES)]
+        if between:
+            between()
         for q in range(PIECES):
-            z_out[k, :, part_of(q)] = place(k, q).astype(bf16)
-            home(k, q).start()
+            if k == 1:
+                z_out[k, :, part_of(q)] = sums[q].astype(bf16)
+                home(k, q).start()
+                continue
+
+            @pl.when(inner == 0)
+            def _():
+                z_out[k, :, part_of(q)] = sums[q].astype(bf16)
+                relay(k, q).start()
+
+            @pl.when(inner == 1)
+            def _():
+                relay(k, q).wait_recv()
+                both = sums[q] + relay_buf[k - 2, :, part_of(q)].astype(f32)
+                z_out[k, :, part_of(q)] = both.astype(bf16)
+                home(k, q).start()
 
     def decode_rows():
         span = keys_buf.shape[0] * tok_rows
@@ -742,11 +771,8 @@
         def _():
             go_home(1)
 
-    @pl.loop(2, 4)
-    def _(k):
-        go_home(k)
-
-    send_back(0)
+    go_home(2)
+    go_home(3, lambda: send_back(0))
     decode_rows()
     for q in range(PIECES):
         here = part_of(q)
@@ -754,9 +780,9 @@
     for q in range(PIECES):
         here = part_of(q)
         result = mixed[:, here]
-        for back in (1, 2, 3):
-            home_in(back, q).wait_recv()
-            result = result + z_in[lax.rem(z + back, 4), :, here].astype(f32)
+        for line in (flip(z, 1), 2 - lax.div(z, 2)):
+            home_in(line, q).wait_recv()
+            result = result + z_in[line, :, here].astype(f32)
         out_ref[:, here] = result.astype(out_ref.dtype)
     for piece in range(2):
         swap(piece).wait_send()
@@ -873,7 +899,8 @@
             pltpu.VMEM(gate_up.shape, bf16),
             pltpu.VMEM(down.shape, bf16),
         ]
-        + [dma((size,)) for size in sizes],
+        + [dma((size,)) for size in sizes]
+        + [pltpu.VMEM((2, tok_rows, half), bf16), dma((2 * PIECES,))],
         compiler_params=pltpu.CompilerParams(
             collective_id=0, has_side_effects=True, vmem_limit_bytes=60 * 1024 * 1024
         ),

time: 101 us -> 96.3 us (0.953)
  Pallas kernels: 95.6 us -> 91 us
    pallas_call x1, Pallas kernels: 95.6 us -> 91 us  [layer(): pl.pallas_call(layer_kernel, out_shape=(jax.ShapeDtypeStruct((tok_rows, h...]
where the time goes in v5:
time: 96.3 us; the launch traced here: 96.1 us
  Pallas kernels  91 us (94%)
  local copies, waits for them, and re-layouts  4.44 us (5%)
    pallas_call x1, Pallas kernels, layer(): pl.pallas_call(layer_kernel, out_shape=(jax.ShapeDtypeStruct((tok_rows, h...  91 us
    unnamed x3, local copies, waits for them, and re-layouts  4.44 us

profile of v5, /device:TPU:0, one launch (start us, length us, event | category | flops | bytes accessed | tf_op | source)
XLA Modules:
  0.0 96.1 jit_solution(7330758037971279405)
XLA Ops:
  0.6 91.0 %shard_map.184 = (bf16[128,1024]{1,0:T(8,128)(2,1)}, bf16[64,512]{1,0:T(8,128)(2,1)}, bf16[4,1024]{1,0:T(4,128)(2,1)}) custom-call(s32[2]{0:T(128)} %req_len_ref.1, s32[2]{0:T(128)} %req_offset_ref.1, f32[1,128]{1,0:T(1,128)} %constant.2.clone.freq_ref, bf16[128,2048]{1,0:T(8,128)(2,1)} %hidden_ref.1, f32[1,2048]{1,0:T(1,128)} %bitcast.17, ...), custom_call_target="tpu_custom_call" | custom-call | tf_op jit(solution)/shard_map/pallas_call | solution.py:863
  91.6 1.7 %copy.23 = bf16[128,1024]{1,0:T(8,128)(2,1)} copy(bf16[128,1024]{1,0:T(8,128)(2,1)} %get-tuple-element.12) | data formatting | bytes 524288
  93.3 1.5 %copy.24 = bf16[4,16,512]{2,1,0:T(8,128)(2,1)} copy(bf16[4,16,512]{2,1,0:T(8,128)(2,1)} %bitcast.16) | data formatting | bytes 131072
  94.8 1.3 %copy.25 = bf16[4,1024]{1,0:T(4,128)(2,1)} copy(bf16[4,1024]{1,0:T(4,128)(2,1)} %get-tuple-element.14) | data formatting | bytes 16384

commit v6 on v5

--- a/solution.py
+++ b/solution.py
@@ -355,6 +355,8 @@
     loads[0].wait()
     loads[1].wait()
     for two in range(heads // 2):
+        if two == heads // 4:
+            key_ring(1)
         left = queries[:, 384 * two : 384 * two + 128]
         middle = queries[:, 384 * two + 128 : 384 * two + 256].astype(f32)
         right = queries[:, 384 * two + 256 : 384 * two + 384].astype(f32)
@@ -394,7 +396,6 @@
         total[part_no, :, :1] = norm
         acc[part_no] = mixture
 
-    key_ring(1)
     meet_keys(0)
     key_ring(2)
     share_keys_in(0).wait_recv()
@@ -635,7 +636,6 @@
         rows_in[k, h, c, :, here] = stage[k, c, :, here]
 
     def meet_rows(k):
-        share(k, 0).start()
         for step in (1, 2, 3):
             for q in range(PIECES):
                 go_in(k, step, q).wait_recv()
@@ -743,6 +743,7 @@
             for q in range(PIECES):
                 ring(t, q)
                 pick(t, q)
+            share(t, 0).start()
 
         @pl.when(t == 0)
         def _():

time: 96.3 us -> 96.2 us (level)
  no operation moved by 1% of the time
where the time goes in v6:
time: 96.2 us; the launch traced here: 96 us
  Pallas kernels  90.9 us (94%)
  local copies, waits for them, and re-layouts  4.44 us (5%)
    pallas_call x1, Pallas kernels, layer(): pl.pallas_call(layer_kernel, out_shape=(jax.ShapeDtypeStruct((tok_rows, h...  90.9 us
    unnamed x3, local copies, waits for them, and re-layouts  4.44 us

profile of v6, /device:TPU:0, one launch (start us, length us, event | category | flops | bytes accessed | tf_op | source)
XLA Modules:
  0.0 96.0 jit_solution(7506897537165890901)
XLA Ops:
  0.6 90.9 %shard_map.184 = (bf16[128,1024]{1,0:T(8,128)(2,1)}, bf16[64,512]{1,0:T(8,128)(2,1)}, bf16[4,1024]{1,0:T(4,128)(2,1)}) custom-call(s32[2]{0:T(128)} %req_len_ref.1, s32[2]{0:T(128)} %req_offset_ref.1, f32[1,128]{1,0:T(1,128)} %constant.2.clone.freq_ref, bf16[128,2048]{1,0:T(8,128)(2,1)} %hidden_ref.1, f32[1,2048]{1,0:T(1,128)} %bitcast.17, ...), custom_call_target="tpu_custom_call" | custom-call | tf_op jit(solution)/shard_map/pallas_call | solution.py:864
  91.5 1.7 %copy.23 = bf16[128,1024]{1,0:T(8,128)(2,1)} copy(bf16[128,1024]{1,0:T(8,128)(2,1)} %get-tuple-element.12) | data formatting | bytes 524288
  93.2 1.5 %copy.24 = bf16[4,16,512]{2,1,0:T(8,128)(2,1)} copy(bf16[4,16,512]{2,1,0:T(8,128)(2,1)} %bitcast.16) | data formatting | bytes 131072
  94.7 1.3 %copy.25 = bf16[4,1024]{1,0:T(4,128)(2,1)} copy(bf16[4,1024]{1,0:T(4,128)(2,1)} %get-tuple-element.14) | data formatting | bytes 16384
